TPU v7x, 512 devices: a whole 4x4x16 slice. The times are simulated.
512 devices in a mesh: gx: 8 (over z_hi, y), gy: 4 (over x), shot: 16 (over z_lo, core).
Axes of the slice: x: 4, y: 4, z: 16 (z_hi: 2, z_lo: 8; z = z_hi * 8 + z_lo), core: 2. Of those that a mesh axis runs over, the one named last changes fastest.
Arguments:
- adj_prev: float32 [16, 256, 64, 256], P('shot', 'gx', 'gy'), may hold values from -6 to 6
- adj_cur: float32 [16, 256, 64, 256], P('shot', 'gx', 'gy'), may hold values from -6 to 6
- fwd_accel: bfloat16 [16, 4, 256, 64, 256], P('shot', None, 'gx', 'gy'), may hold values from -6 to 6
- courant2: float32 [256, 64, 256], P('gx', 'gy'), may hold values from 0.05 to 0.18
- traces: bfloat16 [16, 4, 2048], P('shot', None, ('gx', 'gy')), may hold values from -6 to 6
- weights: bfloat16 [8, 4, 64, 16, 256], P('gx', 'gy'), may hold values from -3 to 3
- rblock: int32 [8, 4, 64], P('gx', 'gy'), may hold values from 0 to 127
- column: int32 [8, 4, 64], P('gx', 'gy'), may hold values from 0 to 511
- counts: int32 [8, 4], P('gx', 'gy'), may hold values from 16 to 64
Outputs:
- adj_prev_out: float32 [16, 256, 64, 256], P('shot', 'gx', 'gy')
- adj_cur_out: float32 [16, 256, 64, 256], P('shot', 'gx', 'gy')
- gradient: float32 [128, 32, 128], P('gx', 'gy')
All inputs are finite; a program needn't handle non-finite values.
Results may differ from a plain program's by a relative error of at most 0.00045.
Values may be sent and summed in bfloat16 or wider, within the bound.
A program may use at most 128 MiB of HBM per device.

v0:
```python
import jax
import jax.numpy as jnp
from jax import lax
from jax.sharding import PartitionSpec as P

LAPLACE_COEFS = (-205.0 / 72.0, 8.0 / 5.0, -1.0 / 5.0, 8.0 / 315.0, -1.0 / 560.0)


def padded_2(array, sides, width):
    edges = {}
    for axis, dim in sides:
        peers, length = (lax.axis_size(axis), array.shape[dim])
        up = [(i, (i + 1) % peers) for i in range(peers - 1)]
        last = lax.slice_in_dim(array, length - width, length, axis=dim)
        initial = lax.slice_in_dim(array, 0, width, axis=dim)
        edges[dim] = (
            lax.ppermute(last, axis, up),
            lax.ppermute(initial, axis, [(b, a) for a, b in up]),
        )
    done = []
    for _, dim in sides:
        low, high = edges[dim]
        around = [(width, width) if d in done else (0, 0) for d in range(array.ndim)]
        array = jnp.concatenate([jnp.pad(low, around), array, jnp.pad(high, around)], axis=dim)
        done.append(dim)
    return array


def laid_out(blocks, dim):
    blocks = jnp.moveaxis(blocks, 0, dim)
    dims = blocks.shape
    return blocks.reshape(*dims[:dim], dims[dim] * dims[dim + 1], *dims[dim + 2 :])


def from_everyone(array, axis):
    copies = jnp.broadcast_to(array, (lax.axis_size(axis), *array.shape))
    return lax.all_to_all(copies, axis, split_axis=0, concat_axis=0, tiled=True)


def gather_directly(array, axis, dim):
    return laid_out(from_everyone(array, axis), dim)


def taken_together(array, axis):
    everything = from_everyone(array, axis)
    return jnp.sum(everything, axis=0)


def laplace_padded(padded_xy, size_x, size_y, size_z):
    padded = jnp.pad(padded_xy, ((0, 0), (0, 0), (4, 4)))
    center = padded[4 : 4 + size_x, 4 : 4 + size_y, 4 : 4 + size_z]
    total = 3.0 * LAPLACE_COEFS[0] * center
    for offset in range(1, 5):
        weight = LAPLACE_COEFS[offset]
        total = total + weight * (
            padded[4 + offset : 4 + offset + size_x, 4 : 4 + size_y, 4 : 4 + size_z]
            + padded[4 - offset : 4 - offset + size_x, 4 : 4 + size_y, 4 : 4 + size_z]
        )
        total = total + weight * (
            padded[4 : 4 + size_x, 4 + offset : 4 + offset + size_y, 4 : 4 + size_z]
            + padded[4 : 4 + size_x, 4 - offset : 4 - offset + size_y, 4 : 4 + size_z]
        )
        total = total + weight * (
            padded[4 : 4 + size_x, 4 : 4 + size_y, 4 + offset : 4 + offset + size_z]
            + padded[4 : 4 + size_x, 4 : 4 + size_y, 4 - offset : 4 - offset + size_z]
        )
    return total


def extend(field):
    return padded_2(field, (("gx", 0), ("gy", 1)), 4)


def restrict(fine):
    size_x, size_y, size_z = fine.shape
    return fine.reshape(size_x // 2, 2, size_y // 2, 2, size_z // 2, 2).mean(axis=(1, 3, 5))


def local(adj_prev, adj_cur, fwd_accel, courant2, traces, weights, rblock, column, counts):
    previous = adj_prev[0]
    current = adj_cur[0]
    size_x, size_y, size_z = current.shape
    steps = fwd_accel.shape[1]
    slots = weights.shape[2]
    recv_block = weights.shape[3]
    gathered = gather_directly(traces, ("gx", "gy"), 2)
    blocks = gathered[0].reshape(steps, -1, recv_block)
    picked = jnp.take(blocks, rblock[0, 0], axis=1)
    contrib = jnp.einsum("tsr,srz->tsz", picked, weights[0, 0], preferred_element_type=jnp.float32)
    live_slots = (jnp.arange(slots, dtype=jnp.int32) < counts[0, 0]).astype(jnp.float32)
    onehot = (
        column[0, 0][:, None] == jnp.arange(size_x * size_y, dtype=jnp.int32)[None, :]
    ).astype(jnp.float32) * live_slots[:, None]
    source = jnp.einsum("sc,tsz->tcz", onehot, contrib, precision=lax.Precision.HIGHEST).reshape(
        steps, size_x, size_y, size_z
    )
    fine = jnp.zeros(current.shape, jnp.float32)
    for step_index in range(steps):
        padded_xy = extend(current)
        next_field = (
            2.0 * current
            - previous
            + courant2 * laplace_padded(padded_xy, size_x, size_y, size_z)
            + source[step_index]
        )
        fine = fine + fwd_accel[0, step_index].astype(jnp.float32) * next_field
        previous, current = (current, next_field)
    gradient = taken_together(restrict(fine), "shot")
    return (previous[None], current[None], gradient)


def solution(mesh):
    return jax.shard_map(
        local,
        mesh=mesh,
        in_specs=(
            P("shot", "gx", "gy", None),
            P("shot", "gx", "gy", None),
            P("shot", None, "gx", "gy", None),
            P("gx", "gy", None),
            P("shot", None, ("gx", "gy")),
            P("gx", "gy", None, None, None),
            P("gx", "gy", None),
            P("gx", "gy", None),
            P("gx", "gy"),
        ),
        out_specs=(P("shot", "gx", "gy", None), P("shot", "gx", "gy", None), P("gx", "gy", None)),
        check_vma=False,
    )
```

profile of v0, /device:TPU:25, one launch (start us, length us, event | category | flops | bytes accessed | tf_op | source)
XLA Modules:
  0.0 260.1 jit_solution(3301277312014826393)
XLA Ops:
  2.1 20.0 %all-to-all-start = ((bf16[32,2,128]{2,1,0:T(2,128)(2,1)}), bf16[32,2,128]{2,1,0:T(2,128)(2,1)S(1)}, u32[]{:S(2)}, u32[]{:S(2)}) async-start(bf16[32,2,128]{2,1,0:T(2,128)(2,1)} %reshape.83), calls=%async_computation | async-start | bytes 32768 | tf_op jit(solution)/shard_map/all_to_all | solution.py:37
  23.0 2.5 collective-permute-start
  25.5 13.6 %collective-permute-start.1 = (f32[4,16,256]{2,1,0:T(8,128)S(1)}, f32[4,16,256]{2,1,0:T(8,128)S(1)}, u32[]{:S(2)}, u32[]{:S(2)}) collective-permute-start(f32[4,16,256]{2,1,0:T(8,128)S(1)} %get-tuple-element.32), channel_id=1, source_target_pairs={{0,64},{64,128},{128,192},{192,256},{256,320},{320,384},{384,448},... | collective-permute-start | bytes 196616 | tf_op jit(solution)/shard_map/ppermute | solution.py:17
  40.2 3.1 %collective-permute-start.3 = (f32[32,4,256]{2,1,0:T(4,128)S(1)}, f32[32,4,256]{2,1,0:T(4,128)S(1)}, u32[]{:S(2)}, u32[]{:S(2)}) collective-permute-start(f32[32,4,256]{2,1,0:T(4,128)S(1)} %get-tuple-element.29), channel_id=1, source_target_pairs={{0,16},{16,32},{32,48},{1,17},{17,33},{33,49},{2,18},{18,34},{34,5... | collective-permute-start | bytes 393224 | tf_op jit(solution)/shard_map/ppermute | solution.py:17
  43.3 1.3 collective-permute-start.2
  47.9 1.9 convolution_bitcast_fusion
  54.0 2.0 fusion.93
  56.0 4.0 %collective-permute-start.7 = (f32[32,4,256]{2,1,0:T(4,128)S(1)}, f32[32,4,256]{2,1,0:T(4,128)S(1)}, u32[]{:S(2)}, u32[]{:S(2)}) collective-permute-start(f32[32,4,256]{2,1,0:T(4,128)S(1)} %get-tuple-element.25), channel_id=1, source_target_pairs={{0,16},{16,32},{32,48},{1,17},{17,33},{33,49},{2,18},{18,34},{34,5... | collective-permute-start | bytes 393224 | tf_op jit(solution)/shard_map/ppermute | solution.py:17
  61.3 1.9 collective-permute-start.4
  63.3 14.2 %collective-permute-start.5 = (f32[4,16,256]{2,1,0:T(8,128)S(1)}, f32[4,16,256]{2,1,0:T(8,128)S(1)}, u32[]{:S(2)}, u32[]{:S(2)}) collective-permute-start(f32[4,16,256]{2,1,0:T(8,128)S(1)} %get-tuple-element.28), channel_id=1, source_target_pairs={{0,64},{64,128},{128,192},{192,256},{256,320},{320,384},{384,448},... | collective-permute-start | bytes 196616 | tf_op jit(solution)/shard_map/ppermute | solution.py:17
  79.8 2.0 fusion.66
  81.9 4.0 %collective-permute-start.11 = (f32[32,4,256]{2,1,0:T(4,128)S(1)}, f32[32,4,256]{2,1,0:T(4,128)S(1)}, u32[]{:S(2)}, u32[]{:S(2)}) collective-permute-start(f32[32,4,256]{2,1,0:T(4,128)S(1)} %get-tuple-element.21), channel_id=1, source_target_pairs={{0,16},{16,32},{32,48},{1,17},{17,33},{33,49},{2,18},{18,34},{34,5... | collective-permute-start | bytes 393224 | tf_op jit(solution)/shard_map/ppermute | solution.py:17
  87.2 1.9 collective-permute-start.8
  89.1 14.5 %collective-permute-start.9 = (f32[4,16,256]{2,1,0:T(8,128)S(1)}, f32[4,16,256]{2,1,0:T(8,128)S(1)}, u32[]{:S(2)}, u32[]{:S(2)}) collective-permute-start(f32[4,16,256]{2,1,0:T(8,128)S(1)} %get-tuple-element.24), channel_id=1, source_target_pairs={{0,64},{64,128},{128,192},{192,256},{256,320},{320,384},{384,448},... | collective-permute-start | bytes 196616 | tf_op jit(solution)/shard_map/ppermute | solution.py:17
  105.9 2.0 fusion.39
  108.0 4.0 %collective-permute-start.15 = (f32[32,4,256]{2,1,0:T(4,128)S(1)}, f32[32,4,256]{2,1,0:T(4,128)S(1)}, u32[]{:S(2)}, u32[]{:S(2)}) collective-permute-start(f32[32,4,256]{2,1,0:T(4,128)S(1)} %get-tuple-element.19), channel_id=1, source_target_pairs={{0,16},{16,32},{32,48},{1,17},{17,33},{33,49},{2,18},{18,34},{34,5... | collective-permute-start | bytes 393224 | tf_op jit(solution)/shard_map/ppermute | solution.py:17
  113.3 14.5 %collective-permute-start.13 = (f32[4,16,256]{2,1,0:T(8,128)S(1)}, f32[4,16,256]{2,1,0:T(8,128)S(1)}, u32[]{:S(2)}, u32[]{:S(2)}) collective-permute-start(f32[4,16,256]{2,1,0:T(8,128)S(1)} %get-tuple-element.17), channel_id=1, source_target_pairs={{0,64},{64,128},{128,192},{192,256},{256,320},{320,384},{384,448},... | collective-permute-start | bytes 196616 | tf_op jit(solution)/shard_map/ppermute | solution.py:17
  127.8 2.1 collective-permute-start.12
  129.9 2.0 copy.34
  132.0 11.6 %collective-permute-done.12 = f32[4,16,256]{2,1,0:T(8,128)S(1)} collective-permute-done((f32[4,16,256]{2,1,0:T(8,128)S(1)}, f32[4,16,256]{2,1,0:T(8,128)S(1)}, u32[]{:S(2)}, u32[]{:S(2)}) %collective-permute-start.12) | collective-permute-done | bytes 65568 | tf_op jit(solution)/shard_map/ppermute | solution.py:18
  145.8 2.9 %fusion.149 = (f32[32,16,256]{2,1,0:T(8,128)S(1)}, f32[32,16,256]{2,1,0:T(8,128)}) fusion(f32[32,16,256]{2,1,0:T(8,128)S(1)} %fusion.39, f32[32,16,256]{2,1,0:T(8,128)S(1)} %fusion.66, f32[32,16,256]{2,1,0:T(8,128)S(1)} %fusion.93, bf16[1,4,32,16,256]{4,3,2,1,0:T(8,128)(2,1)S(1)} %copy-done.5, f32[32,16,256]{2,1,0:T(8,128)S(1)} %bitcast.59, ...), kind=kLoop, calls=%fused_computation.267 | loop fusion | flops 7995392 | bytes 13238272 | tf_op jit(solution)/shard_map/add | solution.py:106
  148.6 34.8 %reshape.69 = f32[16,2,8,2,128,2]{5,4,3,2,1,0:T(8,128)} reshape(f32[32,16,256]{2,1,0:T(8,128)S(1)} %get-tuple-element.3) | data formatting | bytes 1048576 | tf_op jit(solution)/shard_map/reshape | solution.py:76
  183.5 12.2 %reduce_sum.18 = f32[16,8,128]{2,1,0:T(8,128)S(1)} reduce(f32[16,2,8,2,128,2]{5,4,3,2,1,0:T(8,128)} %reshape.69, f32[]{:T(128)} %constant.9.clone.1), dimensions={1,3,5}, to_apply=%region_0.1 | reduce | flops 114688 | bytes 589828 | tf_op jit(solution)/shard_map/reduce_sum | solution.py:76
  195.8 63.6 %all_to_all.10 = f32[16,16,8,128]{3,2,1,0:T(8,128)S(1)} all-to-all(f32[16,16,8,128]{3,2,1,0:T(8,128)S(1)} %broadcast_in_dim.29), channel_id=1, replica_groups=mesh['gx'=8,'gy'=4,'shot'=16] {'shot'}, dimensions={0} | all-to-all | bytes 2097152 | tf_op jit(solution)/shard_map/all_to_all | solution.py:37
  (78 shorter events, 21.6 us)
Async XLA Ops:
  0.6 47.0 %copy-start = (bf16[1,1,64,16,256]{4,3,2,1,0:T(8,128)(2,1)S(1)}, bf16[1,1,64,16,256]{4,3,2,1,0:T(8,128)(2,1)}, u32[]{:S(2)}) copy-start(bf16[1,1,64,16,256]{4,3,2,1,0:T(8,128)(2,1)} %param.14) | copy-start | bytes 1572868
  0.6 47.2 %copy-start.7 = (s32[1,1,64]{2,1,0:T(1,128)S(1)}, s32[1,1,64]{2,1,0:T(1,128)}, u32[]{:S(2)}) copy-start(s32[1,1,64]{2,1,0:T(1,128)} %param.16) | copy-start | bytes 772
  2.1 44.5 %all-to-all-start = ((bf16[32,2,128]{2,1,0:T(2,128)(2,1)}), bf16[32,2,128]{2,1,0:T(2,128)(2,1)S(1)}, u32[]{:S(2)}, u32[]{:S(2)}) async-start(bf16[32,2,128]{2,1,0:T(2,128)(2,1)} %reshape.83), calls=%async_computation | async-start | bytes 32768 | tf_op jit(solution)/shard_map/all_to_all | solution.py:37
  23.0 28.3 %collective-permute-start = (f32[4,16,256]{2,1,0:T(8,128)S(1)}, f32[4,16,256]{2,1,0:T(8,128)S(1)}, u32[]{:S(2)}, u32[]{:S(2)}) collective-permute-start(f32[4,16,256]{2,1,0:T(8,128)S(1)} %get-tuple-element.31), channel_id=1, source_target_pairs={{64,0},{128,64},{192,128},{256,192},{320,256},{384,320},{448,384},... | collective-permute-start | bytes 196616 | tf_op jit(solution)/shard_map/ppermute | solution.py:18
  25.5 25.8 %collective-permute-start.1 = (f32[4,16,256]{2,1,0:T(8,128)S(1)}, f32[4,16,256]{2,1,0:T(8,128)S(1)}, u32[]{:S(2)}, u32[]{:S(2)}) collective-permute-start(f32[4,16,256]{2,1,0:T(8,128)S(1)} %get-tuple-element.32), channel_id=1, source_target_pairs={{0,64},{64,128},{128,192},{192,256},{256,320},{320,384},{384,448},... | collective-permute-start | bytes 196616 | tf_op jit(solution)/shard_map/ppermute | solution.py:17
  40.2 11.0 %collective-permute-start.3 = (f32[32,4,256]{2,1,0:T(4,128)S(1)}, f32[32,4,256]{2,1,0:T(4,128)S(1)}, u32[]{:S(2)}, u32[]{:S(2)}) collective-permute-start(f32[32,4,256]{2,1,0:T(4,128)S(1)} %get-tuple-element.29), channel_id=1, source_target_pairs={{0,16},{16,32},{32,48},{1,17},{17,33},{33,49},{2,18},{18,34},{34,5... | collective-permute-start | bytes 393224 | tf_op jit(solution)/shard_map/ppermute | solution.py:17
  43.3 7.9 %collective-permute-start.2 = (f32[32,4,256]{2,1,0:T(4,128)S(1)}, f32[32,4,256]{2,1,0:T(4,128)S(1)}, u32[]{:S(2)}, u32[]{:S(2)}) collective-permute-start(f32[32,4,256]{2,1,0:T(4,128)S(1)} %get-tuple-element.30), channel_id=1, source_target_pairs={{16,0},{32,16},{48,32},{17,1},{33,17},{49,33},{18,2},{34,18},{50,3... | collective-permute-start | bytes 393224 | tf_op jit(solution)/shard_map/ppermute | solution.py:18
  52.8 1.0 copy-start.3
  52.8 1.2 copy-start.6
  56.0 22.7 %collective-permute-start.7 = (f32[32,4,256]{2,1,0:T(4,128)S(1)}, f32[32,4,256]{2,1,0:T(4,128)S(1)}, u32[]{:S(2)}, u32[]{:S(2)}) collective-permute-start(f32[32,4,256]{2,1,0:T(4,128)S(1)} %get-tuple-element.25), channel_id=1, source_target_pairs={{0,16},{16,32},{32,48},{1,17},{17,33},{33,49},{2,18},{18,34},{34,5... | collective-permute-start | bytes 393224 | tf_op jit(solution)/shard_map/ppermute | solution.py:17
  60.0 18.7 %collective-permute-start.6 = (f32[32,4,256]{2,1,0:T(4,128)S(1)}, f32[32,4,256]{2,1,0:T(4,128)S(1)}, u32[]{:S(2)}, u32[]{:S(2)}) collective-permute-start(f32[32,4,256]{2,1,0:T(4,128)S(1)} %get-tuple-element.26), channel_id=1, source_target_pairs={{16,0},{32,16},{48,32},{17,1},{33,17},{49,33},{18,2},{34,18},{50,3... | collective-permute-start | bytes 393224 | tf_op jit(solution)/shard_map/ppermute | solution.py:18
  61.3 17.5 %collective-permute-start.4 = (f32[4,16,256]{2,1,0:T(8,128)S(1)}, f32[4,16,256]{2,1,0:T(8,128)S(1)}, u32[]{:S(2)}, u32[]{:S(2)}) collective-permute-start(f32[4,16,256]{2,1,0:T(8,128)S(1)} %get-tuple-element.27), channel_id=1, source_target_pairs={{64,0},{128,64},{192,128},{256,192},{320,256},{384,320},{448,384},... | collective-permute-start | bytes 196616 | tf_op jit(solution)/shard_map/ppermute | solution.py:18
  63.3 15.5 %collective-permute-start.5 = (f32[4,16,256]{2,1,0:T(8,128)S(1)}, f32[4,16,256]{2,1,0:T(8,128)S(1)}, u32[]{:S(2)}, u32[]{:S(2)}) collective-permute-start(f32[4,16,256]{2,1,0:T(8,128)S(1)} %get-tuple-element.28), channel_id=1, source_target_pairs={{0,64},{64,128},{128,192},{192,256},{256,320},{320,384},{384,448},... | collective-permute-start | bytes 196616 | tf_op jit(solution)/shard_map/ppermute | solution.py:17
  81.9 23.0 %collective-permute-start.11 = (f32[32,4,256]{2,1,0:T(4,128)S(1)}, f32[32,4,256]{2,1,0:T(4,128)S(1)}, u32[]{:S(2)}, u32[]{:S(2)}) collective-permute-start(f32[32,4,256]{2,1,0:T(4,128)S(1)} %get-tuple-element.21), channel_id=1, source_target_pairs={{0,16},{16,32},{32,48},{1,17},{17,33},{33,49},{2,18},{18,34},{34,5... | collective-permute-start | bytes 393224 | tf_op jit(solution)/shard_map/ppermute | solution.py:17
  85.9 19.0 %collective-permute-start.10 = (f32[32,4,256]{2,1,0:T(4,128)S(1)}, f32[32,4,256]{2,1,0:T(4,128)S(1)}, u32[]{:S(2)}, u32[]{:S(2)}) collective-permute-start(f32[32,4,256]{2,1,0:T(4,128)S(1)} %get-tuple-element.22), channel_id=1, source_target_pairs={{16,0},{32,16},{48,32},{17,1},{33,17},{49,33},{18,2},{34,18},{50,3... | collective-permute-start | bytes 393224 | tf_op jit(solution)/shard_map/ppermute | solution.py:18
  87.2 17.7 %collective-permute-start.8 = (f32[4,16,256]{2,1,0:T(8,128)S(1)}, f32[4,16,256]{2,1,0:T(8,128)S(1)}, u32[]{:S(2)}, u32[]{:S(2)}) collective-permute-start(f32[4,16,256]{2,1,0:T(8,128)S(1)} %get-tuple-element.23), channel_id=1, source_target_pairs={{64,0},{128,64},{192,128},{256,192},{320,256},{384,320},{448,384},... | collective-permute-start | bytes 196616 | tf_op jit(solution)/shard_map/ppermute | solution.py:18
  89.1 15.8 %collective-permute-start.9 = (f32[4,16,256]{2,1,0:T(8,128)S(1)}, f32[4,16,256]{2,1,0:T(8,128)S(1)}, u32[]{:S(2)}, u32[]{:S(2)}) collective-permute-start(f32[4,16,256]{2,1,0:T(8,128)S(1)} %get-tuple-element.24), channel_id=1, source_target_pairs={{0,64},{64,128},{128,192},{192,256},{256,320},{320,384},{384,448},... | collective-permute-start | bytes 196616 | tf_op jit(solution)/shard_map/ppermute | solution.py:17
  107.9 36.7 %copy-start.2 = (f32[32,16,256]{2,1,0:T(8,128)}, f32[32,16,256]{2,1,0:T(8,128)S(1)}, u32[]{:S(2)}) copy-start(f32[32,16,256]{2,1,0:T(8,128)S(1)} %fusion.39) | copy-start | bytes 1572868
  108.0 23.9 %collective-permute-start.15 = (f32[32,4,256]{2,1,0:T(4,128)S(1)}, f32[32,4,256]{2,1,0:T(4,128)S(1)}, u32[]{:S(2)}, u32[]{:S(2)}) collective-permute-start(f32[32,4,256]{2,1,0:T(4,128)S(1)} %get-tuple-element.19), channel_id=1, source_target_pairs={{0,16},{16,32},{32,48},{1,17},{17,33},{33,49},{2,18},{18,34},{34,5... | collective-permute-start | bytes 393224 | tf_op jit(solution)/shard_map/ppermute | solution.py:17
  112.0 20.0 %collective-permute-start.14 = (f32[32,4,256]{2,1,0:T(4,128)S(1)}, f32[32,4,256]{2,1,0:T(4,128)S(1)}, u32[]{:S(2)}, u32[]{:S(2)}) collective-permute-start(f32[32,4,256]{2,1,0:T(4,128)S(1)} %get-tuple-element.20), channel_id=1, source_target_pairs={{16,0},{32,16},{48,32},{17,1},{33,17},{49,33},{18,2},{34,18},{50,3... | collective-permute-start | bytes 393224 | tf_op jit(solution)/shard_map/ppermute | solution.py:18
  113.3 18.7 %collective-permute-start.13 = (f32[4,16,256]{2,1,0:T(8,128)S(1)}, f32[4,16,256]{2,1,0:T(8,128)S(1)}, u32[]{:S(2)}, u32[]{:S(2)}) collective-permute-start(f32[4,16,256]{2,1,0:T(8,128)S(1)} %get-tuple-element.17), channel_id=1, source_target_pairs={{0,64},{64,128},{128,192},{192,256},{256,320},{320,384},{384,448},... | collective-permute-start | bytes 196616 | tf_op jit(solution)/shard_map/ppermute | solution.py:17
  127.8 15.8 %collective-permute-start.12 = (f32[4,16,256]{2,1,0:T(8,128)S(1)}, f32[4,16,256]{2,1,0:T(8,128)S(1)}, u32[]{:S(2)}, u32[]{:S(2)}) collective-permute-start(f32[4,16,256]{2,1,0:T(8,128)S(1)} %get-tuple-element.18), channel_id=1, source_target_pairs={{64,0},{128,64},{192,128},{256,192},{320,256},{384,320},{448,384},... | collective-permute-start | bytes 196616 | tf_op jit(solution)/shard_map/ppermute | solution.py:18
  144.4 1.0 copy-start.4
  144.4 1.4 copy-start.5
  (1 other events, 1.0 us)
where the time goes:
time: 262 us; the launch traced here: 260 us
  starting transfers between devices  105 us (40%)
  blocking collectives  63.6 us (24%)
  local copies, waits for them, and re-layouts  48.6 us (19%)
  other arithmetic  26.8 us (10%)
  waiting for transfers between devices  11.6 us (4%)
    ppermute x8, starting transfers between devices, padded_2(): lax.ppermute(last, axis, up)  71.8 us
    all_to_all x1, blocking collectives, from_everyone(): return lax.all_to_all(copies, axis, split_axis=0, concat_axis=0, tiled=True)  63.6 us
    reshape x1, local copies, waits for them, and re-layouts, restrict(): fine.reshape(size_x // 2, 2, size_y // 2, 2, size_z // 2, 2)  34.8 us
    all_to_all x1, starting transfers between devices, from_everyone(): return lax.all_to_all(copies, axis, split_axis=0, concat_axis=0, tiled=True)  20 us
    ppermute x8, starting transfers between devices, padded_2(): lax.ppermute(initial, axis, [(b, a) for a, b in up])  13.6 us
    reduce_sum x1, other arithmetic, restrict(): fine.reshape(size_x // 2, 2, size_y // 2, 2, size_z // 2, 2)  12.2 us
    ppermute x8, waiting for transfers between devices, padded_2(): lax.ppermute(initial, axis, [(b, a) for a, b in up])  11.6 us
    add x3, other arithmetic, local(): 2.0 * current - previous  6.05 us
  transfers between devices with their start and end apart: 17, of which 1 were waited for; matrix products, arithmetic and copies ran while one was open for 5% of the time, Pallas kernels for 0%

commit v1 on v0

v1 whole, which is shorter than its diff:
```python
import functools

import jax
import jax.numpy as jnp
import ml_dtypes
from jax import lax
from jax.experimental import pallas as pl
from jax.experimental.pallas import tpu as pltpu
from jax.sharding import PartitionSpec as P

MESH = pl.DeviceIdType.MESH
COEFS = (-205.0 / 72.0, 8.0 / 5.0, -1.0 / 5.0, 8.0 / 315.0, -1.0 / 560.0)
F32, BF16, I32 = jnp.float32, jnp.bfloat16, jnp.int32
STEPS, CX, CY, HALF = 4, 32, 16, 128
SLOTS, RB = 64, 16
GX, GY, SHOTS = 8, 4, 16
LO, HI = 0, 1


def iota(shape, dim):
    return lax.broadcasted_iota(I32, shape, dim)


def flag(condition):
    return jnp.where(condition, 1.0, 0.0).astype(F32)


def kernel(
    prev_h, cur_h, acc_h, c2_h, w_h, tr_ref, rb_ref, col_ref, cnt_ref,
    prev_o, cur_o, grad_o,
    field, prev, accel, c2, weights, base, source, fine, packed, band_hi, band_lo,
    halo_y_lo, halo_y_hi, halo_x, send_x, traces, block, spread, onehot, pick, pooled, local, arrived, total,
    in_sem, out_sem, xs_sem, xr_sem, ys_sem, yr_sem, ts_sem, tr_sem, rs_sem, rr_sem, as_sem, ar_sem,
):
    gx, gy, shot = lax.axis_index("gx"), lax.axis_index("gy"), lax.axis_index("shot")
    tile = gx * GY + gy

    def tile_peer(i):
        other = lax.rem(tile + i, GX * GY)
        return {"gx": lax.div(other, GY), "gy": lax.rem(other, GY)}, other

    def shot_peer(i):
        other = lax.rem(shot + i, SHOTS)
        return {"shot": other}, other

    loads = []
    for half in range(2):
        lanes = pl.ds(half * HALF, HALF)
        loads.append(pltpu.make_async_copy(
            cur_h.at[:, :, lanes], field.at[0, half, pl.ds(4, CX), pl.ds(8, CY), :], in_sem.at[half]))
        loads.append(pltpu.make_async_copy(prev_h.at[:, :, lanes], prev.at[half], in_sem.at[2 + half]))
        loads.append(pltpu.make_async_copy(c2_h.at[:, :, lanes], c2.at[half], in_sem.at[4 + half]))
        loads.append(pltpu.make_async_copy(acc_h.at[:, :, :, lanes], accel.at[:, half], in_sem.at[6 + half]))
    loads.append(pltpu.make_async_copy(w_h, weights, in_sem.at[8]))
    for copy in loads:
        copy.start()

    barrier = pltpu.get_barrier_semaphore()

    def greet_tile(i, carry):
        pl.semaphore_signal(barrier, 1, device_id=tile_peer(i)[0], device_id_type=MESH)
        return carry

    def greet_shot(i, carry):
        pl.semaphore_signal(barrier, 1, device_id=shot_peer(i)[0], device_id_type=MESH)
        return carry

    lax.fori_loop(1, GX * GY, greet_tile, 0)
    lax.fori_loop(1, SHOTS, greet_shot, 0)

    zero_rows = jnp.zeros((CX, 8, HALF), F32)
    zero_planes = jnp.zeros((4, 32, HALF), F32)
    for t in range(STEPS):
        for half in range(2):
            field[t, half, pl.ds(0, 4), :, :] = zero_planes
            field[t, half, pl.ds(4 + CX, 4), :, :] = zero_planes
            field[t, half, pl.ds(4, CX), pl.ds(0, 8), :] = zero_rows
            field[t, half, pl.ds(4, CX), pl.ds(24, 8), :] = zero_rows
            halo_y_lo[t, half, :, pl.ds(8, 8), :] = zero_rows
            halo_y_hi[t, half, :, pl.ds(0, 8), :] = zero_rows

    @pl.when(gx == 0)
    def _():
        halo_x[:, LO] = jnp.zeros((STEPS, 2, 5, CY, HALF), BF16)

    @pl.when(gx == GX - 1)
    def _():
        halo_x[:, HI] = jnp.zeros((STEPS, 2, 5, CY, HALF), BF16)

    @pl.when(gy == 0)
    def _():
        for t in range(STEPS):
            for half in range(2):
                halo_y_lo[t, half, :, pl.ds(0, 8), :] = zero_rows

    @pl.when(gy == GY - 1)
    def _():
        for t in range(STEPS):
            for half in range(2):
                halo_y_hi[t, half, :, pl.ds(8, 8), :] = zero_rows

    block[...] = jnp.zeros((8, HALF), F32)
    block[pl.ds(0, STEPS), pl.ds(0, 64)] = tr_ref[0].astype(F32)
    as_is = block[...]
    turned = pltpu.roll(as_is, 64, 1)
    traces[tile, pl.ds(0, 1), :] = as_is[0:1] + turned[1:2]
    traces[tile, pl.ds(1, 1), :] = as_is[2:3] + turned[3:4]

    distance = jnp.abs(iota((256, 256), 0) - iota((256, 256), 1))
    band = jnp.zeros((256, 256), F32)
    rest = jnp.zeros((256, 256), F32)
    for k in range(1, 5):
        high = float(ml_dtypes.bfloat16(COEFS[k]))
        band = jnp.where(distance == k, high, band)
        rest = jnp.where(distance == k, COEFS[k] - high, rest)
    band_hi[pl.ds(0, 256), :] = band.astype(BF16)
    band_hi[pl.ds(256, 256), :] = band.astype(BF16)
    band_lo[...] = rest.astype(BF16)

    spread[...] = flag((iota((128, 1024), 0) & 15) == (iota((128, 1024), 1) & 15)).astype(BF16)
    slot_row = iota((1, SLOTS), 1)
    live = slot_row < cnt_ref[...]
    hit = flag((iota((CX * CY, SLOTS), 0) == col_ref[...]) & live).astype(BF16)
    onehot[...] = jnp.concatenate([hit, hit], axis=1)
    diagonal = iota((SLOTS, SLOTS), 0) == iota((SLOTS, SLOTS), 1)
    rb_column = jnp.sum(jnp.where(diagonal, rb_ref[...].astype(F32), 0.0), axis=1, keepdims=True).astype(I32)
    pick[...] = flag((rb_column >> 2) == iota((SLOTS, 32), 1))
    quarter = rb_column & 3

    for copy in loads[0:8:4]:
        copy.wait()

    def pack_edge(t, half, x, value):
        high = value.astype(BF16)
        if x < 4:
            send_x[t, LO, half, x] = high
            if x == 0:
                send_x[t, LO, half, 4] = (value - high.astype(F32)).astype(BF16)
        if x >= CX - 4:
            send_x[t, HI, half, x - (CX - 4)] = high
            if x == CX - 1:
                send_x[t, HI, half, 4] = (value - high.astype(F32)).astype(BF16)

    def split(half, x, value):
        high = value.astype(BF16)
        packed[x, :, pl.ds(half * HALF, HALF)] = high
        packed[x, :, pl.ds(256 + half * HALF, HALF)] = (value - high.astype(F32)).astype(BF16)

    def x_copy(t, side):
        return pltpu.make_async_remote_copy(
            src_ref=send_x.at[t, 1 - side], dst_ref=halo_x.at[t, side],
            send_sem=xs_sem.at[t, side], recv_sem=xr_sem.at[t, side],
            device_id={"gx": gx + 1 if side == LO else gx - 1}, device_id_type=MESH)

    def y_copy(t, side):
        if side == LO:
            src = field.at[t, :, pl.ds(4, CX), pl.ds(20, 4), :]
            dst = halo_y_lo.at[t, :, :, pl.ds(4, 4), :]
        else:
            src = field.at[t, :, pl.ds(4, CX), pl.ds(8, 4), :]
            dst = halo_y_hi.at[t, :, :, pl.ds(8, 4), :]
        return pltpu.make_async_remote_copy(
            src_ref=src, dst_ref=dst, send_sem=ys_sem.at[t, side], recv_sem=yr_sem.at[t, side],
            device_id={"gy": gy + 1 if side == LO else gy - 1}, device_id_type=MESH)

    sends_x = {LO: gx < GX - 1, HI: gx > 0}
    gets_x = {LO: gx > 0, HI: gx < GX - 1}
    sends_y = {LO: gy < GY - 1, HI: gy > 0}
    gets_y = {LO: gy > 0, HI: gy < GY - 1}

    def each(conditions, make, t, act):
        for side in (LO, HI):
            @pl.when(conditions[side])
            def _():
                getattr(make(t, side), act)()

    EDGES = (0, 1, 2, 3, CX - 4, CX - 3, CX - 2, CX - 1)
    for half in range(2):
        for x in EDGES:
            pack_edge(0, half, x, field[0, half, 4 + x, pl.ds(8, CY), :])

    pl.semaphore_wait(barrier, GX * GY - 1 + SHOTS - 1)

    each(sends_x, x_copy, 0, "start")

    def trace_copy(i):
        peer, _ = tile_peer(i)
        return pltpu.make_async_remote_copy(
            src_ref=traces.at[tile, pl.ds(0, 2)], dst_ref=traces.at[tile, pl.ds(0, 2)],
            send_sem=ts_sem.at[i], recv_sem=tr_sem.at[tile], device_id=peer, device_id_type=MESH)

    def start_trace(i, carry):
        trace_copy(i).start()
        return carry

    lax.fori_loop(1, GX * GY, start_trace, 0)
    each(sends_y, y_copy, 0, "start")

    def split_plane(x, carry):
        for half in range(2):
            split(half, x, field[0, half, 4 + x, pl.ds(8, CY), :])
        return carry

    lax.fori_loop(0, CX, split_plane, 0)
    for i in (1, 2, 3, 5, 6, 7, 8):
        loads[i].wait()

    def base_step(t):
        def chunk(c, carry):
            x0 = pl.multiple_of(c * 8, 8)
            both = packed[pl.ds(x0, 8)].reshape(128, 512)
            along_z = jnp.dot(both, band_hi[...], preferred_element_type=F32)
            along_z += jnp.dot(both[:, :256], band_lo[...], preferred_element_type=F32)
            for half in range(2):
                planes = [field[t, half, x0 + j, pl.ds(8, CY), :] for j in range(16)]
                for i in range(8):
                    center = planes[i + 4]
                    lap = along_z[i * CY : (i + 1) * CY, half * HALF : (half + 1) * HALF] + (3.0 * COEFS[0]) * center
                    for k in range(1, 5):
                        lap += COEFS[k] * (
                            (planes[i + 4 - k] + planes[i + 4 + k])
                            + (field[t, half, x0 + 4 + i, pl.ds(8 - k, CY), :] + field[t, half, x0 + 4 + i, pl.ds(8 + k, CY), :]))
                    if t == 0:
                        before = prev[half, x0 + i]
                    else:
                        before = field[t - 1, half, x0 + 4 + i, pl.ds(8, CY), :] - source[t, half, x0 + i]
                    base[half, x0 + i] = 2.0 * center - before + c2[half, x0 + i] * lap
            return carry

        lax.fori_loop(0, CX // 8, chunk, 0)

    def fix_plane(t, half, x, across):
        low = high = None
        for k in range(1, 5):
            a = COEFS[k] * halo_y_lo[t, half, x, pl.ds(8 - k, 8), :]
            b = COEFS[k] * halo_y_hi[t, half, x, pl.ds(k, 8), :]
            low, high = (a, b) if low is None else (low + a, high + b)
        lap = jnp.concatenate([low, high], axis=0)
        if across is not None:
            lap += across
        value = base[half, x] + c2[half, x] * lap
        if t == 0:
            value += source[0, half, x]
        field[t + 1, half, 4 + x, pl.ds(8, CY), :] = value
        if t < STEPS - 1:
            split(half, x, value)
        product = accel[t, half, x].astype(F32) * value
        fine[half, x] = product if t == 0 else fine[half, x] + product
        return value

    def fix_edges(t, side):
        for half in range(2):
            layer = [halo_x[t, side, half, j].astype(F32) for j in range(4)]
            near = 3 if side == LO else 0
            layer[near] += halo_x[t, side, half, 4].astype(F32)
            for j in range(4):
                x = j if side == LO else CX - 1 - j
                across = None
                for k in range(j + 1, 5):
                    away = k - j - 1
                    term = COEFS[k] * layer[3 - away if side == LO else away]
                    across = term if across is None else across + term
                value = fix_plane(t, half, x, across)
                if t < STEPS - 1:
                    pack_edge(t + 1, half, x, value)

    def fix_middle(t):
        def plane(x, carry):
            for half in range(2):
                fix_plane(t, half, x, None)
            return carry

        lax.fori_loop(4, CX - 4, plane, 0)

    def make_source(t):
        row, odd = t // 2, t % 2
        rows = traces[:, row, :]
        got = jnp.dot(pick[...].astype(BF16), rows.astype(BF16), preferred_element_type=F32)
        lane = iota((SLOTS, HALF), 1)
        keep = ((lane >> 6) == odd) & (((lane >> 4) & 3) == quarter)
        got = jnp.where(keep, got, 0.0).astype(BF16)
        wide = jnp.dot(got, spread[...], preferred_element_type=F32)
        own = (iota((SLOTS, 1024), 1) >> 4) == iota((SLOTS, 1024), 0)
        wide = jnp.where(own, wide, 0.0).astype(BF16)
        contribution = jnp.dot(wide, weights[...], preferred_element_type=F32)
        high = contribution.astype(BF16)
        low = (contribution - high.astype(F32)).astype(BF16)
        stacked = jnp.concatenate([high, low], axis=0)
        dense = jnp.dot(onehot[...], stacked, preferred_element_type=F32)
        for half in range(2):
            source[t, half] = dense[:, half * HALF : (half + 1) * HALF].reshape(CX, CY, HALF)

    base_step(0)

    def wait_trace(i, carry):
        _, other = tile_peer(i)
        pltpu.make_async_remote_copy(
            src_ref=traces.at[other, pl.ds(0, 2)], dst_ref=traces.at[other, pl.ds(0, 2)],
            send_sem=ts_sem.at[i], recv_sem=tr_sem.at[other], device_id=tile_peer(i)[0], device_id_type=MESH).wait_recv()
        return carry

    lax.fori_loop(1, GX * GY, wait_trace, 0)
    make_source(0)

    for t in range(STEPS):
        each(gets_y, y_copy, t, "wait_recv")
        each(gets_x, x_copy, t, "wait_recv")
        fix_edges(t, LO)
        fix_edges(t, HI)
        if t < STEPS - 1:
            each(sends_x, x_copy, t + 1, "start")
        fix_middle(t)
        if t < STEPS - 1:
            each(sends_y, y_copy, t + 1, "start")
            make_source(t + 1)
            base_step(t + 1)

    outs = []
    for half in range(2):
        lanes = pl.ds(half * HALF, HALF)
        for n, (t, out) in enumerate(((STEPS - 1, prev_o), (STEPS, cur_o))):
            outs.append(pltpu.make_async_copy(
                field.at[t, half, pl.ds(4, CX), pl.ds(8, CY), :], out.at[:, :, lanes], out_sem.at[2 * half + n]))
    for copy in outs:
        copy.start()

    pairs = [(fine[half].reshape(CX // 2, 2, CY, HALF)) for half in range(2)]
    pairs = [(p[:, 0] + p[:, 1]).reshape(CX // 2 * CY, HALF) for p in pairs]
    both = jnp.concatenate(pairs, axis=1)
    pool = (flag((iota((256, 128), 0) >> 1) == iota((256, 128), 1)) * 0.125).astype(BF16)
    high = both.astype(BF16)
    left = both - high.astype(F32)
    mid = left.astype(BF16)
    last = (left - mid.astype(F32)).astype(BF16)
    pooled[...] = (
        jnp.dot(high, pool, preferred_element_type=F32)
        + jnp.dot(mid, pool, preferred_element_type=F32)
        + jnp.dot(last, pool, preferred_element_type=F32))
    coarse = pooled[pl.ds(0, 128, stride=2), :] + pooled[pl.ds(1, 128, stride=2), :]
    local[...] = coarse.reshape(CX // 2, 8, HALF)

    def row_copy(i, index_of_peer=False):
        peer, other = shot_peer(i)
        return pltpu.make_async_remote_copy(
            src_ref=local.at[other], dst_ref=arrived.at[shot],
            send_sem=rs_sem.at[i], recv_sem=rr_sem.at[shot], device_id=peer, device_id_type=MESH)

    def start_row(i, carry):
        row_copy(i).start()
        return carry

    lax.fori_loop(1, SHOTS, start_row, 0)
    arrived[shot] = local[shot]

    def wait_row(i, carry):
        peer, other = shot_peer(i)
        pltpu.make_async_remote_copy(
            src_ref=local.at[other], dst_ref=arrived.at[other],
            send_sem=rs_sem.at[i], recv_sem=rr_sem.at[other], device_id=peer, device_id_type=MESH).wait_recv()
        return carry

    lax.fori_loop(1, SHOTS, wait_row, 0)
    total[shot] = jnp.sum(arrived[...], axis=0)

    def sum_copy(i):
        peer, _ = shot_peer(i)
        return pltpu.make_async_remote_copy(
            src_ref=total.at[shot], dst_ref=total.at[shot],
            send_sem=as_sem.at[i], recv_sem=ar_sem.at[shot], device_id=peer, device_id_type=MESH)

    def start_sum(i, carry):
        sum_copy(i).start()
        return carry

    lax.fori_loop(1, SHOTS, start_sum, 0)

    def end_trace(i, carry):
        trace_copy(i).wait_send()
        return carry

    lax.fori_loop(1, GX * GY, end_trace, 0)
    for t in range(STEPS):
        each(sends_x, x_copy, t, "wait_send")
        each(sends_y, y_copy, t, "wait_send")

    def wait_sum(i, carry):
        peer, other = shot_peer(i)
        pltpu.make_async_remote_copy(
            src_ref=total.at[other], dst_ref=total.at[other],
            send_sem=as_sem.at[i], recv_sem=ar_sem.at[other], device_id=peer, device_id_type=MESH).wait_recv()
        return carry

    lax.fori_loop(1, SHOTS, wait_sum, 0)
    last_copy = pltpu.make_async_copy(total, grad_o, out_sem.at[4])
    last_copy.start()

    def end_rows(i, carry):
        row_copy(i).wait_send()
        sum_copy(i).wait_send()
        return carry

    lax.fori_loop(1, SHOTS, end_rows, 0)
    for copy in outs:
        copy.wait()
    last_copy.wait()


def local_part(adj_prev, adj_cur, fwd_accel, courant2, traces, weights, rblock, column, counts):
    tile = (CX, CY, 2 * HALF)
    any_ = pl.BlockSpec(memory_space=pl.ANY)
    vmem = pl.BlockSpec(memory_space=pltpu.VMEM)
    dma = pltpu.SemaphoreType.DMA
    previous, current, gradient = pl.pallas_call(
        kernel,
        out_shape=(
            jax.ShapeDtypeStruct(tile, F32),
            jax.ShapeDtypeStruct(tile, F32),
            jax.ShapeDtypeStruct((CX // 2, CY // 2, HALF), F32),
        ),
        in_specs=[any_] * 5 + [vmem] * 4,
        out_specs=(any_, any_, any_),
        scratch_shapes=[
            pltpu.VMEM((STEPS + 1, 2, CX + 8, 32, HALF), F32),
            pltpu.VMEM((2, CX, CY, HALF), F32),
            pltpu.VMEM((STEPS, 2, CX, CY, HALF), BF16),
            pltpu.VMEM((2, CX, CY, HALF), F32),
            pltpu.VMEM((SLOTS * RB, 256), BF16),
            pltpu.VMEM((2, CX, CY, HALF), F32),
            pltpu.VMEM((STEPS, 2, CX, CY, HALF), F32),
            pltpu.VMEM((2, CX, CY, HALF), F32),
            pltpu.VMEM((CX, CY, 512), BF16),
            pltpu.VMEM((512, 256), BF16),
            pltpu.VMEM((256, 256), BF16),
            pltpu.VMEM((STEPS, 2, CX, 16, HALF), F32),
            pltpu.VMEM((STEPS, 2, CX, 16, HALF), F32),
            pltpu.VMEM((STEPS, 2, 2, 5, CY, HALF), BF16),
            pltpu.VMEM((STEPS, 2, 2, 5, CY, HALF), BF16),
            pltpu.VMEM((GX * GY, 8, HALF), F32),
            pltpu.VMEM((8, HALF), F32),
            pltpu.VMEM((128, 1024), BF16),
            pltpu.VMEM((CX * CY, 2 * SLOTS), BF16),
            pltpu.VMEM((SLOTS, 32), F32),
            pltpu.VMEM((256, HALF), F32),
            pltpu.VMEM((CX // 2, 8, HALF), F32),
            pltpu.VMEM((SHOTS, 8, HALF), F32),
            pltpu.VMEM((CX // 2, 8, HALF), F32),
            dma((9,)), dma((5,)),
            dma((STEPS, 2)), dma((STEPS, 2)), dma((STEPS, 2)), dma((STEPS, 2)),
            dma((GX * GY,)), dma((GX * GY,)),
            dma((SHOTS,)), dma((SHOTS,)), dma((SHOTS,)), dma((SHOTS,)),
        ],
        compiler_params=pltpu.CompilerParams(
            collective_id=0, has_side_effects=True, vmem_limit_bytes=48 << 20),
    )(
        adj_prev[0], adj_cur[0], fwd_accel[0], courant2, weights[0, 0].reshape(SLOTS * RB, 256),
        traces, rblock[0], column[0], counts,
    )
    return previous[None], current[None], gradient


def solution(mesh):
    return jax.shard_map(
        local_part,
        mesh=mesh,
        in_specs=(
            P("shot", "gx", "gy", None),
            P("shot", "gx", "gy", None),
            P("shot", None, "gx", "gy", None),
            P("gx", "gy", None),
            P("shot", None, ("gx", "gy")),
            P("gx", "gy", None, None, None),
            P("gx", "gy", None),
            P("gx", "gy", None),
            P("gx", "gy"),
        ),
        out_specs=(P("shot", "gx", "gy", None), P("shot", "gx", "gy", None), P("gx", "gy", None)),
        check_vma=False,
    )
```

time: 262 us -> 84.4 us (0.32)
  starting transfers between devices: 105 us -> 0 us
  Pallas kernels: 0 us -> 74.4 us
  blocking collectives: 63.6 us -> 0 us
  local copies, waits for them, and re-layouts: 48.6 us -> 8.28 us
  other arithmetic: 26.8 us -> 0 us
  waiting for transfers between devices: 11.6 us -> 0 us
    ppermute x16 -> x0, starting transfers between devices: 85.4 us -> none  [the longest x8 71.8 us: padded_2(): lax.ppermute(last, axis, up)]
    pallas_call x0 -> x1, Pallas kernels: none -> 74.4 us  [local_part(): pl.pallas_call(kernel, out_shape=(jax.ShapeDtypeStruct(tile, F32), jax.Sh...]
    all_to_all x1 -> x0, blocking collectives: 63.6 us -> none  [from_everyone(): return lax.all_to_all(copies, axis, split_axis=0, concat_axis=0, tiled=True)]
    reshape x1 -> x0, local copies, waits for them, and re-layouts: 34.8 us -> none  [restrict(): fine.reshape(size_x // 2, 2, size_y // 2, 2, size_z // 2, 2)]
    all_to_all x1 -> x0, starting transfers between devices: 20 us -> none  [from_everyone(): return lax.all_to_all(copies, axis, split_axis=0, concat_axis=0, tiled=True)]
    reduce_sum x2 -> x0, other arithmetic: 12.9 us -> none  [the longest x1 12.2 us: restrict(): fine.reshape(size_x // 2, 2, size_y // 2, 2, size_z // 2, 2)]
    ppermute x16 -> x0, waiting for transfers between devices: 11.6 us -> none  [the longest x8 11.6 us: padded_2(): lax.ppermute(initial, axis, [(b, a) for a, b in up])]
    add x4 -> x0, other arithmetic: 8.92 us -> none  [the longest x3 6.05 us: local(): 2.0 * current - previous]
  transfers between devices with their start and end apart: 17 -> 0, of which waited for: 1 -> 0; matrix products, arithmetic and copies ran while one was open for 5% -> 0% of each run, Pallas kernels for 0% -> 0%
where the time goes in v1:
time: 84.4 us; the launch traced here: 84 us
  Pallas kernels  74.4 us (88%)
  local copies, waits for them, and re-layouts  8.28 us (10%)
  between operations  1.32 us (2%)
    pallas_call x1, Pallas kernels, local_part(): pl.pallas_call(kernel, out_shape=(jax.ShapeDtypeStruct(tile, F32), jax.Sh...  74.4 us
    unnamed x19, local copies, waits for them, and re-layouts  8.28 us

profile of v1, /device:TPU:25, one launch (start us, length us, event | category | flops | bytes accessed | tf_op | source)
XLA Modules:
  0.0 84.0 jit_solution(10426702971832200179)
XLA Ops:
  1.3 0.0 copy-start.7
  1.3 0.0 copy-start.5
  1.3 0.0 copy-start.6
  1.3 0.6 copy-done.7
  1.9 0.0 copy-done.5
  2.0 0.0 copy-done.6
  2.0 0.0 copy-start
  2.0 1.2 %copy-done = bf16[1,4,32,16,256]{4,3,2,1,0:T(8,128)(2,1)S(1)} copy-done((bf16[1,4,32,16,256]{4,3,2,1,0:T(8,128)(2,1)S(1)}, bf16[1,4,32,16,256]{4,3,2,1,0:T(8,128)(2,1)}, u32[]{:S(2)}) %copy-start) | copy-done | bytes 1048600
  3.2 0.0 copy-start.1
  3.2 1.0 %copy-done.1 = f32[1,32,16,256]{3,2,1,0:T(8,128)S(1)} copy-done((f32[1,32,16,256]{3,2,1,0:T(8,128)S(1)}, f32[1,32,16,256]{3,2,1,0:T(8,128)}, u32[]{:S(2)}) %copy-start.1) | copy-done | bytes 524312
  4.2 0.0 copy-start.2
  4.2 1.0 %copy-done.2 = f32[1,32,16,256]{3,2,1,0:T(8,128)S(1)} copy-done((f32[1,32,16,256]{3,2,1,0:T(8,128)S(1)}, f32[1,32,16,256]{3,2,1,0:T(8,128)}, u32[]{:S(2)}) %copy-start.2) | copy-done | bytes 524312
  5.3 0.0 copy-start.3
  5.3 1.0 %copy-done.3 = f32[32,16,256]{2,1,0:T(8,128)S(1)} copy-done((f32[32,16,256]{2,1,0:T(8,128)S(1)}, f32[32,16,256]{2,1,0:T(8,128)}, u32[]{:S(2)}) %copy-start.3) | copy-done | bytes 524312
  6.3 0.0 copy-start.4
  6.3 1.0 %copy-done.4 = bf16[1,1,64,16,256]{4,3,2,1,0:T(8,128)(2,1)S(1)} copy-done((bf16[1,1,64,16,256]{4,3,2,1,0:T(8,128)(2,1)S(1)}, bf16[1,1,64,16,256]{4,3,2,1,0:T(8,128)(2,1)}, u32[]{:S(2)}) %copy-start.4) | copy-done | bytes 524312
  7.4 74.4 %shard_map.112 = (f32[32,16,256]{2,1,0:T(8,128)S(1)}, f32[32,16,256]{2,1,0:T(8,128)S(1)}, f32[16,8,128]{2,1,0:T(8,128)S(1)}) custom-call(f32[32,16,256]{2,1,0:T(8,128)S(1)} %bitcast.11, f32[32,16,256]{2,1,0:T(8,128)S(1)} %bitcast.12, bf16[4,32,16,256]{3,2,1,0:T(8,128)(2,1)S(1)} %bitcast.8, f32[32,16,256]{2,1,0:T(8,128)S(1)} %copy-done.3, ...), custom_call_target="tpu_custom_call" | custom-call | tf_op jit(solution)/shard_map/pallas_call | solution.py:413
  81.8 0.8 copy.16
  82.6 0.8 copy.17
  83.4 0.6 copy.18
Async XLA Ops:
  1.3 0.7 copy-start.7
  1.3 0.7 copy-start.5
  1.3 0.7 copy-start.6
  2.0 1.2 %copy-start = (bf16[1,4,32,16,256]{4,3,2,1,0:T(8,128)(2,1)S(1)}, bf16[1,4,32,16,256]{4,3,2,1,0:T(8,128)(2,1)}, u32[]{:S(2)}) copy-start(bf16[1,4,32,16,256]{4,3,2,1,0:T(8,128)(2,1)} %param.11) | copy-start | bytes 3145732
  3.2 1.0 %copy-start.1 = (f32[1,32,16,256]{3,2,1,0:T(8,128)S(1)}, f32[1,32,16,256]{3,2,1,0:T(8,128)}, u32[]{:S(2)}) copy-start(f32[1,32,16,256]{3,2,1,0:T(8,128)} %param.9) | copy-start | bytes 1572868
  4.2 1.0 %copy-start.2 = (f32[1,32,16,256]{3,2,1,0:T(8,128)S(1)}, f32[1,32,16,256]{3,2,1,0:T(8,128)}, u32[]{:S(2)}) copy-start(f32[1,32,16,256]{3,2,1,0:T(8,128)} %param.10) | copy-start | bytes 1572868
  5.3 1.0 %copy-start.3 = (f32[32,16,256]{2,1,0:T(8,128)S(1)}, f32[32,16,256]{2,1,0:T(8,128)}, u32[]{:S(2)}) copy-start(f32[32,16,256]{2,1,0:T(8,128)} %c2_h.1) | copy-start | bytes 1572868
  6.3 1.0 %copy-start.4 = (bf16[1,1,64,16,256]{4,3,2,1,0:T(8,128)(2,1)S(1)}, bf16[1,1,64,16,256]{4,3,2,1,0:T(8,128)(2,1)}, u32[]{:S(2)}) copy-start(bf16[1,1,64,16,256]{4,3,2,1,0:T(8,128)(2,1)} %param.14) | copy-start | bytes 1572868

commit v2 on v1

--- a/solution.py
+++ b/solution.py
@@ -15,6 +15,7 @@
 SLOTS, RB = 64, 16
 GX, GY, SHOTS = 8, 4, 16
 LO, HI = 0, 1
+PARTS = 4
 
 
 def iota(shape, dim):
@@ -26,22 +27,49 @@
 
 
 def kernel(
-    prev_h, cur_h, acc_h, c2_h, w_h, tr_ref, rb_ref, col_ref, cnt_ref,
+    prev_h, cur_h, acc_h, c2_h, w_h, tr_h, rb_h, col_h, cnt_h,
     prev_o, cur_o, grad_o,
-    field, prev, accel, c2, weights, base, source, fine, packed, band_hi, band_lo,
-    halo_y_lo, halo_y_hi, halo_x, send_x, traces, block, spread, onehot, pick, pooled, local, arrived, total,
-    in_sem, out_sem, xs_sem, xr_sem, ys_sem, yr_sem, ts_sem, tr_sem, rs_sem, rr_sem, as_sem, ar_sem,
+    field, prev, accel, c2, weights, tr_ref, rb_ref, col_ref, cnt_ref,
+    base, source, fine, packed, band_hi, band_lo, halo_y_lo, halo_y_hi, halo_x, send_x,
+    traces, block, spread, onehot, pick, pooled, local, arrived, arrived_edge, total, final,
+    in_sem, xs_sem, xr_sem, ys_sem, yr_sem, zs_sem, zr_sem, ts_sem, tr_sem, rs_sem, rr_sem, es_sem, er_sem, as_sem, ar_sem, bs_sem, out_sem,
 ):
     gx, gy, shot = lax.axis_index("gx"), lax.axis_index("gy"), lax.axis_index("shot")
-    tile = gx * GY + gy
-
-    def tile_peer(i):
-        other = lax.rem(tile + i, GX * GY)
-        return {"gx": lax.div(other, GY), "gy": lax.rem(other, GY)}, other
+    z_hi, row = lax.div(gx, 4), lax.rem(gx, 4)
+    spot = row * 4 + gy
+
+    def spot_peer(i):
+        other = lax.rem(spot + i, 16)
+        return {"gx": z_hi * 4 + lax.div(other, 4), "gy": lax.rem(other, 4)}, other
+
+    partner = {"gx": lax.rem(gx + 4, GX)}
+    faces_half = (gx == 3) | (gx == 4)
 
     def shot_peer(i):
         other = lax.rem(shot + i, SHOTS)
         return {"shot": other}, other
+
+    barrier = pltpu.get_barrier_semaphore()
+
+    def greet(device):
+        pl.semaphore_signal(barrier, 1, device_id=device, device_id_type=MESH)
+
+    greet(partner)
+
+    @pl.when(faces_half)
+    def _():
+        greet({"gx": 7 - gx})
+
+    def greet_shot(i, carry):
+        greet(shot_peer(i)[0])
+        return carry
+
+    def greet_spot(i, carry):
+        greet(spot_peer(i)[0])
+        return carry
+
+    lax.fori_loop(1, SHOTS, greet_shot, 0)
+    lax.fori_loop(1, 16, greet_spot, 0)
 
     loads = []
     for half in range(2):
@@ -52,21 +80,10 @@
         loads.append(pltpu.make_async_copy(c2_h.at[:, :, lanes], c2.at[half], in_sem.at[4 + half]))
         loads.append(pltpu.make_async_copy(acc_h.at[:, :, :, lanes], accel.at[:, half], in_sem.at[6 + half]))
     loads.append(pltpu.make_async_copy(w_h, weights, in_sem.at[8]))
+    for n, (src, dst) in enumerate(((tr_h, tr_ref), (rb_h, rb_ref), (col_h, col_ref), (cnt_h, cnt_ref))):
+        loads.append(pltpu.make_async_copy(src, dst, in_sem.at[9 + n]))
     for copy in loads:
         copy.start()
-
-    barrier = pltpu.get_barrier_semaphore()
-
-    def greet_tile(i, carry):
-        pl.semaphore_signal(barrier, 1, device_id=tile_peer(i)[0], device_id_type=MESH)
-        return carry
-
-    def greet_shot(i, carry):
-        pl.semaphore_signal(barrier, 1, device_id=shot_peer(i)[0], device_id_type=MESH)
-        return carry
-
-    lax.fori_loop(1, GX * GY, greet_tile, 0)
-    lax.fori_loop(1, SHOTS, greet_shot, 0)
 
     zero_rows = jnp.zeros((CX, 8, HALF), F32)
     zero_planes = jnp.zeros((4, 32, HALF), F32)
@@ -99,12 +116,15 @@
             for half in range(2):
                 halo_y_hi[t, half, :, pl.ds(8, 8), :] = zero_rows
 
+    for copy in loads[9:]:
+        copy.wait()
+
     block[...] = jnp.zeros((8, HALF), F32)
     block[pl.ds(0, STEPS), pl.ds(0, 64)] = tr_ref[0].astype(F32)
     as_is = block[...]
     turned = pltpu.roll(as_is, 64, 1)
-    traces[tile, pl.ds(0, 1), :] = as_is[0:1] + turned[1:2]
-    traces[tile, pl.ds(1, 1), :] = as_is[2:3] + turned[3:4]
+    traces[spot, z_hi, pl.ds(0, 1), :] = as_is[0:1] + turned[1:2]
+    traces[spot, z_hi, pl.ds(1, 1), :] = as_is[2:3] + turned[3:4]
 
     distance = jnp.abs(iota((256, 256), 0) - iota((256, 256), 1))
     band = jnp.zeros((256, 256), F32)
@@ -124,7 +144,8 @@
     onehot[...] = jnp.concatenate([hit, hit], axis=1)
     diagonal = iota((SLOTS, SLOTS), 0) == iota((SLOTS, SLOTS), 1)
     rb_column = jnp.sum(jnp.where(diagonal, rb_ref[...].astype(F32), 0.0), axis=1, keepdims=True).astype(I32)
-    pick[...] = flag((rb_column >> 2) == iota((SLOTS, 32), 1))
+    holder = rb_column >> 2
+    pick[...] = flag(((holder & 15) * 2 + (holder >> 4)) == iota((SLOTS, 32), 1))
     quarter = rb_column & 3
 
     for copy in loads[0:8:4]:
@@ -178,23 +199,6 @@
     for half in range(2):
         for x in EDGES:
             pack_edge(0, half, x, field[0, half, 4 + x, pl.ds(8, CY), :])
-
-    pl.semaphore_wait(barrier, GX * GY - 1 + SHOTS - 1)
-
-    each(sends_x, x_copy, 0, "start")
-
-    def trace_copy(i):
-        peer, _ = tile_peer(i)
-        return pltpu.make_async_remote_copy(
-            src_ref=traces.at[tile, pl.ds(0, 2)], dst_ref=traces.at[tile, pl.ds(0, 2)],
-            send_sem=ts_sem.at[i], recv_sem=tr_sem.at[tile], device_id=peer, device_id_type=MESH)
-
-    def start_trace(i, carry):
-        trace_copy(i).start()
-        return carry
-
-    lax.fori_loop(1, GX * GY, start_trace, 0)
-    each(sends_y, y_copy, 0, "start")
 
     def split_plane(x, carry):
         for half in range(2):
@@ -241,9 +245,11 @@
         value = base[half, x] + c2[half, x] * lap
         if t == 0:
             value += source[0, half, x]
-        field[t + 1, half, 4 + x, pl.ds(8, CY), :] = value
         if t < STEPS - 1:
+            field[t + 1, half, 4 + x, pl.ds(8, CY), :] = value
             split(half, x, value)
+        if t == STEPS - 1:
+            final[half, x] = value
         product = accel[t, half, x].astype(F32) * value
         fine[half, x] = product if t == 0 else fine[half, x] + product
         return value
@@ -273,8 +279,8 @@
         lax.fori_loop(4, CX - 4, plane, 0)
 
     def make_source(t):
-        row, odd = t // 2, t % 2
-        rows = traces[:, row, :]
+        at, odd = t // 2, t % 2
+        rows = traces[:, :, at, :].reshape(32, HALF)
         got = jnp.dot(pick[...].astype(BF16), rows.astype(BF16), preferred_element_type=F32)
         lane = iota((SLOTS, HALF), 1)
         keep = ((lane >> 6) == odd) & (((lane >> 4) & 3) == quarter)
@@ -292,117 +298,231 @@
 
     base_step(0)
 
+    pl.semaphore_wait(barrier, 31 + faces_half.astype(I32))
+
+    def send_traces():
+        return pltpu.make_async_remote_copy(
+            src_ref=traces.at[spot, z_hi, pl.ds(0, 2)], dst_ref=traces.at[spot, z_hi, pl.ds(0, 2)],
+            send_sem=zs_sem.at[0], recv_sem=zr_sem.at[0], device_id=partner, device_id_type=MESH)
+
+    def get_traces():
+        return pltpu.make_async_remote_copy(
+            src_ref=traces.at[spot, 1 - z_hi, pl.ds(0, 2)], dst_ref=traces.at[spot, 1 - z_hi, pl.ds(0, 2)],
+            send_sem=zs_sem.at[0], recv_sem=zr_sem.at[0], device_id=partner, device_id_type=MESH)
+
+    def pass_traces(i):
+        peer, _ = spot_peer(i)
+        return pltpu.make_async_remote_copy(
+            src_ref=traces.at[spot, :, pl.ds(0, 2)], dst_ref=traces.at[spot, :, pl.ds(0, 2)],
+            send_sem=ts_sem.at[i], recv_sem=tr_sem.at[spot], device_id=peer, device_id_type=MESH)
+
+    send_traces().start()
+    each(sends_x, x_copy, 0, "start")
+    each(sends_y, y_copy, 0, "start")
+    get_traces().wait_recv()
+
+    def start_trace(i, carry):
+        pass_traces(i).start()
+        return carry
+
+    lax.fori_loop(1, 16, start_trace, 0)
+
     def wait_trace(i, carry):
-        _, other = tile_peer(i)
+        peer, other = spot_peer(i)
         pltpu.make_async_remote_copy(
-            src_ref=traces.at[other, pl.ds(0, 2)], dst_ref=traces.at[other, pl.ds(0, 2)],
-            send_sem=ts_sem.at[i], recv_sem=tr_sem.at[other], device_id=tile_peer(i)[0], device_id_type=MESH).wait_recv()
+            src_ref=traces.at[other, :, pl.ds(0, 2)], dst_ref=traces.at[other, :, pl.ds(0, 2)],
+            send_sem=ts_sem.at[i], recv_sem=tr_sem.at[other], device_id=peer, device_id_type=MESH).wait_recv()
         return carry
 
-    lax.fori_loop(1, GX * GY, wait_trace, 0)
+    lax.fori_loop(1, 16, wait_trace, 0)
     make_source(0)
 
+    pool = (flag((iota((256, 128), 0) >> 1) == iota((256, 128), 1)) * 0.125).astype(BF16)
+
+    def restrict(first, rows):
+        pairs = []
+        for half in range(2):
+            planes = fine[half, pl.ds(2 * first, 2 * rows)].reshape(rows, 2, CY, HALF)
+            pairs.append((planes[:, 0] + planes[:, 1]).reshape(rows * CY, HALF))
+        both = jnp.concatenate(pairs, axis=1)
+        high = both.astype(BF16)
+        left = both - high.astype(F32)
+        mid = left.astype(BF16)
+        last = (left - mid.astype(F32)).astype(BF16)
+        pooled[pl.ds(0, rows * CY), :] = (
+            jnp.dot(high, pool, preferred_element_type=F32)
+            + jnp.dot(mid, pool, preferred_element_type=F32)
+            + jnp.dot(last, pool, preferred_element_type=F32))
+        size = rows * CY // 2
+        coarse = pooled[pl.ds(0, size, stride=2), :] + pooled[pl.ds(1, size, stride=2), :]
+        local[pl.ds(first, rows)] = coarse.reshape(rows, 8, HALF)
+
+    EDGE_ROWS = (0, 1, CX // 2 - 2, CX // 2 - 1)
+    owns = (shot >= 2) & (shot < SHOTS - 2)
+    owns_edge = (shot >= 6) & (shot < 10)
+    edge_row = jnp.where(shot < 8, shot - 6, shot + 6)
+
+    def row_copy(r, source_shot):
+        return pltpu.make_async_remote_copy(
+            src_ref=local.at[r], dst_ref=arrived.at[source_shot],
+            send_sem=rs_sem.at[r], recv_sem=rr_sem.at[source_shot], device_id={"shot": r}, device_id_type=MESH)
+
+    def edge_copy(e, source_shot):
+        return pltpu.make_async_remote_copy(
+            src_ref=local.at[EDGE_ROWS[e]], dst_ref=arrived_edge.at[source_shot],
+            send_sem=es_sem.at[e], recv_sem=er_sem.at[source_shot], device_id={"shot": 6 + e}, device_id_type=MESH)
+
+    def sum_copy(i, r, sems):
+        peer, _ = shot_peer(i)
+        return pltpu.make_async_remote_copy(
+            src_ref=total.at[r], dst_ref=total.at[r],
+            send_sem=sems.at[i], recv_sem=ar_sem.at[r], device_id=peer, device_id_type=MESH)
+
+    def rows_do(act):
+        def one(r, carry):
+            @pl.when(r != shot)
+            def _():
+                getattr(row_copy(r, shot), act)()
+            return carry
+
+        lax.fori_loop(2, SHOTS - 2, one, 0)
+
+    def edges_do(act):
+        for e in range(4):
+            @pl.when(shot != 6 + e)
+            def _():
+                getattr(edge_copy(e, shot), act)()
+
+    def sums_do(r, sems, act):
+        def one(i, carry):
+            getattr(sum_copy(i, r, sems), act)()
+            return carry
+
+        lax.fori_loop(1, SHOTS, one, 0)
+
+    outs = []
+    for half in range(2):
+        lanes = pl.ds(half * HALF, HALF)
+        outs.append(pltpu.make_async_copy(
+            field.at[STEPS - 1, half, pl.ds(4, CX), pl.ds(8, CY), :], prev_o.at[:, :, lanes], out_sem.at[half]))
+    for half in range(2):
+        lanes = pl.ds(half * HALF, HALF)
+        outs.append(pltpu.make_async_copy(final.at[half], cur_o.at[:, :, lanes], out_sem.at[2 + half]))
+
     for t in range(STEPS):
+        last_step = t == STEPS - 1
         each(gets_y, y_copy, t, "wait_recv")
+        if t > 0:
+            fix_middle(t)
+        if last_step:
+            restrict(2, CX // 2 - 4)
+            rows_do("start")
         each(gets_x, x_copy, t, "wait_recv")
         fix_edges(t, LO)
         fix_edges(t, HI)
-        if t < STEPS - 1:
+        if not last_step:
             each(sends_x, x_copy, t + 1, "start")
-        fix_middle(t)
-        if t < STEPS - 1:
+        if t == 0:
+            fix_middle(t)
+        if t == STEPS - 2:
+            for copy in outs[:2]:
+                copy.start()
+        if not last_step:
             each(sends_y, y_copy, t + 1, "start")
             make_source(t + 1)
             base_step(t + 1)
 
-    outs = []
-    for half in range(2):
-        lanes = pl.ds(half * HALF, HALF)
-        for n, (t, out) in enumerate(((STEPS - 1, prev_o), (STEPS, cur_o))):
-            outs.append(pltpu.make_async_copy(
-                field.at[t, half, pl.ds(4, CX), pl.ds(8, CY), :], out.at[:, :, lanes], out_sem.at[2 * half + n]))
-    for copy in outs:
+    restrict(0, 2)
+    restrict(CX // 2 - 2, 2)
+    edges_do("start")
+    for copy in outs[2:]:
         copy.start()
 
-    pairs = [(fine[half].reshape(CX // 2, 2, CY, HALF)) for half in range(2)]
-    pairs = [(p[:, 0] + p[:, 1]).reshape(CX // 2 * CY, HALF) for p in pairs]
-    both = jnp.concatenate(pairs, axis=1)
-    pool = (flag((iota((256, 128), 0) >> 1) == iota((256, 128), 1)) * 0.125).astype(BF16)
-    high = both.astype(BF16)
-    left = both - high.astype(F32)
-    mid = left.astype(BF16)
-    last = (left - mid.astype(F32)).astype(BF16)
-    pooled[...] = (
-        jnp.dot(high, pool, preferred_element_type=F32)
-        + jnp.dot(mid, pool, preferred_element_type=F32)
-        + jnp.dot(last, pool, preferred_element_type=F32))
-    coarse = pooled[pl.ds(0, 128, stride=2), :] + pooled[pl.ds(1, 128, stride=2), :]
-    local[...] = coarse.reshape(CX // 2, 8, HALF)
-
-    def row_copy(i, index_of_peer=False):
-        peer, other = shot_peer(i)
-        return pltpu.make_async_remote_copy(
-            src_ref=local.at[other], dst_ref=arrived.at[shot],
-            send_sem=rs_sem.at[i], recv_sem=rr_sem.at[shot], device_id=peer, device_id_type=MESH)
-
-    def start_row(i, carry):
-        row_copy(i).start()
+    @pl.when(owns)
+    def _():
+        arrived[shot] = local[shot]
+
+        def wait_row(i, carry):
+            _, other = shot_peer(i)
+            row_copy(shot, other).wait_recv()
+            return carry
+
+        lax.fori_loop(1, SHOTS, wait_row, 0)
+        total[shot] = jnp.sum(arrived[...], axis=0)
+        sums_do(shot, as_sem, "start")
+
+    @pl.when(owns_edge)
+    def _():
+        arrived_edge[shot] = local[edge_row]
+
+        def wait_edge(i, carry):
+            _, other = shot_peer(i)
+            edge_copy(0, other).wait_recv()
+            return carry
+
+        lax.fori_loop(1, SHOTS, wait_edge, 0)
+        total[edge_row] = jnp.sum(arrived_edge[...], axis=0)
+        sums_do(edge_row, bs_sem, "start")
+
+    send_traces().wait_send()
+
+    def end_trace(i, carry):
+        pass_traces(i).wait_send()
         return carry
 
-    lax.fori_loop(1, SHOTS, start_row, 0)
-    arrived[shot] = local[shot]
-
-    def wait_row(i, carry):
-        peer, other = shot_peer(i)
-        pltpu.make_async_remote_copy(
-            src_ref=local.at[other], dst_ref=arrived.at[other],
-            send_sem=rs_sem.at[i], recv_sem=rr_sem.at[other], device_id=peer, device_id_type=MESH).wait_recv()
-        return carry
-
-    lax.fori_loop(1, SHOTS, wait_row, 0)
-    total[shot] = jnp.sum(arrived[...], axis=0)
-
-    def sum_copy(i):
-        peer, _ = shot_peer(i)
-        return pltpu.make_async_remote_copy(
-            src_ref=total.at[shot], dst_ref=total.at[shot],
-            send_sem=as_sem.at[i], recv_sem=ar_sem.at[shot], device_id=peer, device_id_type=MESH)
-
-    def start_sum(i, carry):
-        sum_copy(i).start()
-        return carry
-
-    lax.fori_loop(1, SHOTS, start_sum, 0)
-
-    def end_trace(i, carry):
-        trace_copy(i).wait_send()
-        return carry
-
-    lax.fori_loop(1, GX * GY, end_trace, 0)
+    lax.fori_loop(1, 16, end_trace, 0)
     for t in range(STEPS):
         each(sends_x, x_copy, t, "wait_send")
         each(sends_y, y_copy, t, "wait_send")
-
-    def wait_sum(i, carry):
-        peer, other = shot_peer(i)
-        pltpu.make_async_remote_copy(
-            src_ref=total.at[other], dst_ref=total.at[other],
-            send_sem=as_sem.at[i], recv_sem=ar_sem.at[other], device_id=peer, device_id_type=MESH).wait_recv()
+    rows_do("wait_send")
+    edges_do("wait_send")
+
+    def wait_sum(r, carry):
+        @pl.when(r != shot)
+        def _():
+            sum_copy(1, r, as_sem).wait_recv()
         return carry
 
-    lax.fori_loop(1, SHOTS, wait_sum, 0)
-    last_copy = pltpu.make_async_copy(total, grad_o, out_sem.at[4])
-    last_copy.start()
-
-    def end_rows(i, carry):
-        row_copy(i).wait_send()
-        sum_copy(i).wait_send()
-        return carry
-
-    lax.fori_loop(1, SHOTS, end_rows, 0)
+    lax.fori_loop(2, SHOTS - 2, wait_sum, 0)
+    for e, r in enumerate(EDGE_ROWS):
+        @pl.when(shot != 6 + e)
+        def _():
+            sum_copy(1, r, as_sem).wait_recv()
+
+    last = pltpu.make_async_copy(total, grad_o, out_sem.at[4])
+    last.start()
     for copy in outs:
         copy.wait()
-    last_copy.wait()
+
+    @pl.when(owns)
+    def _():
+        sums_do(shot, as_sem, "wait_send")
+
+    @pl.when(owns_edge)
+    def _():
+        sums_do(edge_row, bs_sem, "wait_send")
+
+    last.wait()
+
+
+def hand_over(prev_i, cur_i, grad_i, prev_o, cur_o, grad_o, held, held_grad, in_sem, out_sem):
+    steps = []
+    for n in range(2 * PARTS):
+        src, dst = ((prev_i, prev_o), (cur_i, cur_o))[n // PARTS]
+        part = pl.ds(n % PARTS * (CX // PARTS), CX // PARTS)
+        steps.append((
+            pltpu.make_async_copy(src.at[part], held.at[n], in_sem.at[n]),
+            pltpu.make_async_copy(held.at[n], dst.at[part], out_sem.at[n])))
+    steps.append((
+        pltpu.make_async_copy(grad_i, held_grad, in_sem.at[2 * PARTS]),
+        pltpu.make_async_copy(held_grad, grad_o, out_sem.at[2 * PARTS])))
+    for get, _ in steps:
+        get.start()
+    for get, put in steps:
+        get.wait()
+        put.start()
+    for _, put in steps:
+        put.wait()
 
 
 def local_part(adj_prev, adj_cur, fwd_accel, courant2, traces, weights, rblock, column, counts):
@@ -410,14 +530,15 @@
     any_ = pl.BlockSpec(memory_space=pl.ANY)
     vmem = pl.BlockSpec(memory_space=pltpu.VMEM)
     dma = pltpu.SemaphoreType.DMA
-    previous, current, gradient = pl.pallas_call(
+    results = (
+        jax.ShapeDtypeStruct(tile, F32),
+        jax.ShapeDtypeStruct(tile, F32),
+        jax.ShapeDtypeStruct((CX // 2, CY // 2, HALF), F32),
+    )
+    made = pl.pallas_call(
         kernel,
-        out_shape=(
-            jax.ShapeDtypeStruct(tile, F32),
-            jax.ShapeDtypeStruct(tile, F32),
-            jax.ShapeDtypeStruct((CX // 2, CY // 2, HALF), F32),
-        ),
-        in_specs=[any_] * 5 + [vmem] * 4,
+        out_shape=results,
+        in_specs=[any_] * 8 + [pl.BlockSpec(memory_space=pltpu.HBM)],
         out_specs=(any_, any_, any_),
         scratch_shapes=[
             pltpu.VMEM((STEPS + 1, 2, CX + 8, 32, HALF), F32),
@@ -425,6 +546,10 @@
             pltpu.VMEM((STEPS, 2, CX, CY, HALF), BF16),
             pltpu.VMEM((2, CX, CY, HALF), F32),
             pltpu.VMEM((SLOTS * RB, 256), BF16),
+            pltpu.VMEM((1, STEPS, 64), BF16),
+            pltpu.VMEM((1, SLOTS), I32),
+            pltpu.VMEM((1, SLOTS), I32),
+            pltpu.VMEM((1, 1), I32),
             pltpu.VMEM((2, CX, CY, HALF), F32),
             pltpu.VMEM((STEPS, 2, CX, CY, HALF), F32),
             pltpu.VMEM((2, CX, CY, HALF), F32),
@@ -435,26 +560,40 @@
             pltpu.VMEM((STEPS, 2, CX, 16, HALF), F32),
             pltpu.VMEM((STEPS, 2, 2, 5, CY, HALF), BF16),
             pltpu.VMEM((STEPS, 2, 2, 5, CY, HALF), BF16),
-            pltpu.VMEM((GX * GY, 8, HALF), F32),
+            pltpu.VMEM((16, 2, 8, HALF), F32),
             pltpu.VMEM((8, HALF), F32),
             pltpu.VMEM((128, 1024), BF16),
             pltpu.VMEM((CX * CY, 2 * SLOTS), BF16),
             pltpu.VMEM((SLOTS, 32), F32),
-            pltpu.VMEM((256, HALF), F32),
+            pltpu.VMEM((192, HALF), F32),
             pltpu.VMEM((CX // 2, 8, HALF), F32),
             pltpu.VMEM((SHOTS, 8, HALF), F32),
+            pltpu.VMEM((SHOTS, 8, HALF), F32),
             pltpu.VMEM((CX // 2, 8, HALF), F32),
-            dma((9,)), dma((5,)),
+            pltpu.VMEM((2, CX, CY, HALF), F32),
+            dma((13,)),
             dma((STEPS, 2)), dma((STEPS, 2)), dma((STEPS, 2)), dma((STEPS, 2)),
-            dma((GX * GY,)), dma((GX * GY,)),
-            dma((SHOTS,)), dma((SHOTS,)), dma((SHOTS,)), dma((SHOTS,)),
+            dma((1,)), dma((1,)), dma((16,)), dma((16,)),
+            dma((SHOTS,)), dma((SHOTS,)), dma((4,)), dma((SHOTS,)), dma((SHOTS,)), dma((SHOTS,)), dma((SHOTS,)), dma((5,)),
         ],
         compiler_params=pltpu.CompilerParams(
-            collective_id=0, has_side_effects=True, vmem_limit_bytes=48 << 20),
+            collective_id=0, has_side_effects=True, vmem_limit_bytes=56 << 20),
     )(
         adj_prev[0], adj_cur[0], fwd_accel[0], courant2, weights[0, 0].reshape(SLOTS * RB, 256),
         traces, rblock[0], column[0], counts,
     )
+    previous, current, gradient = pl.pallas_call(
+        hand_over,
+        out_shape=results,
+        in_specs=[any_] * 3,
+        out_specs=(any_,) * 3,
+        scratch_shapes=[
+            pltpu.VMEM((2 * PARTS, CX // PARTS, CY, 2 * HALF), F32),
+            pltpu.VMEM((CX // 2, CY // 2, HALF), F32),
+            dma((2 * PARTS + 1,)), dma((2 * PARTS + 1,)),
+        ],
+        compiler_params=pltpu.CompilerParams(vmem_limit_bytes=56 << 20),
+    )(*made)
     return previous[None], current[None], gradient
 
 

time: 84.4 us -> 69.6 us (0.82)
  local copies, waits for them, and re-layouts: 8.28 us -> 0 us
  Pallas kernels: 74.4 us -> 68.1 us
    unnamed x19 -> x0, local copies, waits for them, and re-layouts: 8.28 us -> none
    pallas_call x1 -> x2, Pallas kernels: 74.4 us -> 68.1 us  [the longest x1 66 us: local_part(): pl.pallas_call(kernel, out_shape=results, in_specs=[any_] * 8 + [pl.Block...]
where the time goes in v2:
time: 69.6 us; the launch traced here: 69.4 us
  Pallas kernels  68.1 us (98%)
  between operations  1.29 us (2%)
    pallas_call x1, Pallas kernels, local_part(): pl.pallas_call(kernel, out_shape=results, in_specs=[any_] * 8 + [pl.Block...  66 us
    pallas_call x1, Pallas kernels, local_part(): pl.pallas_call(hand_over, out_shape=results, in_specs=[any_] * 3, out_spe...  2.12 us

profile of v2, /device:TPU:25, one launch (start us, length us, event | category | flops | bytes accessed | tf_op | source)
XLA Modules:
  0.0 69.4 jit_solution(17181361117149831473)
XLA Ops:
  1.3 66.0 %shard_map.112 = (f32[32,16,256]{2,1,0:T(8,128)}, f32[32,16,256]{2,1,0:T(8,128)}, f32[16,8,128]{2,1,0:T(8,128)}) custom-call(f32[32,16,256]{2,1,0:T(8,128)} %bitcast.9, f32[32,16,256]{2,1,0:T(8,128)} %bitcast.10, bf16[4,32,16,256]{3,2,1,0:T(8,128)(2,1)} %bitcast.8, f32[32,16,256]{2,1,0:T(8,128)} %c2_h.1, bf16[1024,256]{1,0:T(8,128)(2,1)} %bitcast.11, ...), custom_call_target="tpu_custom_call" | custom-call | tf_op jit(solution)/shard_map/pallas_call | solution.py:538
  67.3 2.1 %shard_map.113 = (f32[32,16,256]{2,1,0:T(8,128)}, f32[32,16,256]{2,1,0:T(8,128)}, f32[16,8,128]{2,1,0:T(8,128)}) custom-call(f32[32,16,256]{2,1,0:T(8,128)} %get-tuple-element.9.prev_i, f32[32,16,256]{2,1,0:T(8,128)} %get-tuple-element.10.cur_i, f32[16,8,128]{2,1,0:T(8,128)} %get-tuple-element.11.grad_i), custom_call_target="tpu_custom_call" | custom-call | tf_op jit(solution)/shard_map/pallas_call | solution.py:585

commit v3 on v2

--- a/solution.py
+++ b/solution.py
@@ -31,8 +31,8 @@
     prev_o, cur_o, grad_o,
     field, prev, accel, c2, weights, tr_ref, rb_ref, col_ref, cnt_ref,
     base, source, fine, packed, band_hi, band_lo, halo_y_lo, halo_y_hi, halo_x, send_x,
-    traces, block, spread, onehot, pick, pooled, local, arrived, arrived_edge, total, final,
-    in_sem, xs_sem, xr_sem, ys_sem, yr_sem, zs_sem, zr_sem, ts_sem, tr_sem, rs_sem, rr_sem, es_sem, er_sem, as_sem, ar_sem, bs_sem, out_sem,
+    traces, block, spread, onehot, pick, pooled, local, arrived, from_twin, late_rows, total,
+    in_sem, xs_sem, xr_sem, ys_sem, yr_sem, zs_sem, zr_sem, ts_sem, tr_sem, rs_sem, rr_sem, es_sem, er_sem, as_sem, ar_sem, bs_sem, br_sem,
 ):
     gx, gy, shot = lax.axis_index("gx"), lax.axis_index("gy"), lax.axis_index("shot")
     z_hi, row = lax.div(gx, 4), lax.rem(gx, 4)
@@ -248,8 +248,8 @@
         if t < STEPS - 1:
             field[t + 1, half, 4 + x, pl.ds(8, CY), :] = value
             split(half, x, value)
-        if t == STEPS - 1:
-            final[half, x] = value
+        if t >= STEPS - 2:
+            (prev_o if t == STEPS - 2 else cur_o)[x, :, pl.ds(half * HALF, HALF)] = value
         product = accel[t, half, x].astype(F32) * value
         fine[half, x] = product if t == 0 else fine[half, x] + product
         return value
@@ -357,112 +357,111 @@
         coarse = pooled[pl.ds(0, size, stride=2), :] + pooled[pl.ds(1, size, stride=2), :]
         local[pl.ds(first, rows)] = coarse.reshape(rows, 8, HALF)
 
-    EDGE_ROWS = (0, 1, CX // 2 - 2, CX // 2 - 1)
-    owns = (shot >= 2) & (shot < SHOTS - 2)
-    owns_edge = (shot >= 6) & (shot < 10)
-    edge_row = jnp.where(shot < 8, shot - 6, shot + 6)
-
-    def row_copy(r, source_shot):
-        return pltpu.make_async_remote_copy(
-            src_ref=local.at[r], dst_ref=arrived.at[source_shot],
-            send_sem=rs_sem.at[r], recv_sem=rr_sem.at[source_shot], device_id={"shot": r}, device_id_type=MESH)
-
-    def edge_copy(e, source_shot):
-        return pltpu.make_async_remote_copy(
-            src_ref=local.at[EDGE_ROWS[e]], dst_ref=arrived_edge.at[source_shot],
-            send_sem=es_sem.at[e], recv_sem=er_sem.at[source_shot], device_id={"shot": 6 + e}, device_id_type=MESH)
-
-    def sum_copy(i, r, sems):
+    late = jnp.where(gx < GX // 2, CX // 2 - 2, 0)
+    early = jnp.where(gx < GX // 2, 0, 2)
+    OWNERS = range(4, 11)
+    owns = (shot >= OWNERS[0]) & (shot <= OWNERS[-1])
+    core = lax.rem(shot, 2)
+    twin = {"shot": shot + 1 - 2 * core}
+
+    def pair_of(owner):
+        return pl.ds(early + 2 * (owner - OWNERS[0]), 2)
+
+    def row_copy(owner, source_shot):
+        return pltpu.make_async_remote_copy(
+            src_ref=local.at[pair_of(owner)], dst_ref=arrived.at[source_shot],
+            send_sem=rs_sem.at[owner], recv_sem=rr_sem.at[source_shot], device_id={"shot": owner}, device_id_type=MESH)
+
+    def sum_copy(i, owner):
         peer, _ = shot_peer(i)
         return pltpu.make_async_remote_copy(
-            src_ref=total.at[r], dst_ref=total.at[r],
-            send_sem=sems.at[i], recv_sem=ar_sem.at[r], device_id=peer, device_id_type=MESH)
+            src_ref=total.at[pair_of(owner)], dst_ref=total.at[pair_of(owner)],
+            send_sem=as_sem.at[i], recv_sem=ar_sem.at[owner], device_id=peer, device_id_type=MESH)
+
+    def twin_copy():
+        return pltpu.make_async_remote_copy(
+            src_ref=local.at[late + 1 - core], dst_ref=from_twin,
+            send_sem=es_sem.at[0], recv_sem=er_sem.at[0], device_id=twin, device_id_type=MESH)
+
+    def late_copy(i, source_shot):
+        peer, _ = shot_peer(i)
+        return pltpu.make_async_remote_copy(
+            src_ref=late_rows.at[source_shot], dst_ref=late_rows.at[source_shot],
+            send_sem=bs_sem.at[i], recv_sem=br_sem.at[source_shot], device_id=peer, device_id_type=MESH)
 
     def rows_do(act):
-        def one(r, carry):
-            @pl.when(r != shot)
+        for owner in OWNERS:
+            @pl.when(owner != shot)
             def _():
-                getattr(row_copy(r, shot), act)()
+                getattr(row_copy(owner, shot), act)()
+
+    def shots_do(make, act):
+        def one(i, carry):
+            getattr(make(i), act)()
             return carry
 
-        lax.fori_loop(2, SHOTS - 2, one, 0)
-
-    def edges_do(act):
-        for e in range(4):
-            @pl.when(shot != 6 + e)
-            def _():
-                getattr(edge_copy(e, shot), act)()
-
-    def sums_do(r, sems, act):
-        def one(i, carry):
-            getattr(sum_copy(i, r, sems), act)()
-            return carry
-
         lax.fori_loop(1, SHOTS, one, 0)
 
-    outs = []
-    for half in range(2):
-        lanes = pl.ds(half * HALF, HALF)
-        outs.append(pltpu.make_async_copy(
-            field.at[STEPS - 1, half, pl.ds(4, CX), pl.ds(8, CY), :], prev_o.at[:, :, lanes], out_sem.at[half]))
-    for half in range(2):
-        lanes = pl.ds(half * HALF, HALF)
-        outs.append(pltpu.make_async_copy(final.at[half], cur_o.at[:, :, lanes], out_sem.at[2 + half]))
-
-    for t in range(STEPS):
-        last_step = t == STEPS - 1
+    for t in range(STEPS - 1):
         each(gets_y, y_copy, t, "wait_recv")
         if t > 0:
             fix_middle(t)
-        if last_step:
-            restrict(2, CX // 2 - 4)
-            rows_do("start")
         each(gets_x, x_copy, t, "wait_recv")
         fix_edges(t, LO)
         fix_edges(t, HI)
-        if not last_step:
-            each(sends_x, x_copy, t + 1, "start")
+        each(sends_x, x_copy, t + 1, "start")
         if t == 0:
             fix_middle(t)
-        if t == STEPS - 2:
-            for copy in outs[:2]:
-                copy.start()
-        if not last_step:
-            each(sends_y, y_copy, t + 1, "start")
-            make_source(t + 1)
-            base_step(t + 1)
-
-    restrict(0, 2)
-    restrict(CX // 2 - 2, 2)
-    edges_do("start")
-    for copy in outs[2:]:
-        copy.start()
+        each(sends_y, y_copy, t + 1, "start")
+        make_source(t + 1)
+        base_step(t + 1)
+
+    t = STEPS - 1
+    each(gets_y, y_copy, t, "wait_recv")
+    fix_middle(t)
+
+    def edge(side):
+        @pl.when(gets_x[side])
+        def _():
+            x_copy(t, side).wait_recv()
+
+        fix_edges(t, side)
+
+    lower = gx < GX // 2
+
+    @pl.when(lower)
+    def _():
+        edge(LO)
+        restrict(0, CX // 2 - 2)
+
+    @pl.when(jnp.logical_not(lower))
+    def _():
+        edge(HI)
+        restrict(2, CX // 2 - 2)
+
+    rows_do("start")
+
+    @pl.when(lower)
+    def _():
+        edge(HI)
+        restrict(CX // 2 - 2, 2)
+
+    @pl.when(jnp.logical_not(lower))
+    def _():
+        edge(LO)
+        restrict(0, 2)
+
+    twin_copy().start()
+    twin_copy().wait_recv()
+    late_rows[shot] = local[late + core] + from_twin[...]
+    shots_do(lambda i: late_copy(i, shot), "start")
 
     @pl.when(owns)
     def _():
-        arrived[shot] = local[shot]
-
-        def wait_row(i, carry):
-            _, other = shot_peer(i)
-            row_copy(shot, other).wait_recv()
-            return carry
-
-        lax.fori_loop(1, SHOTS, wait_row, 0)
-        total[shot] = jnp.sum(arrived[...], axis=0)
-        sums_do(shot, as_sem, "start")
-
-    @pl.when(owns_edge)
-    def _():
-        arrived_edge[shot] = local[edge_row]
-
-        def wait_edge(i, carry):
-            _, other = shot_peer(i)
-            edge_copy(0, other).wait_recv()
-            return carry
-
-        lax.fori_loop(1, SHOTS, wait_edge, 0)
-        total[edge_row] = jnp.sum(arrived_edge[...], axis=0)
-        sums_do(edge_row, bs_sem, "start")
+        arrived[shot] = local[pair_of(shot)]
+        shots_do(lambda i: row_copy(shot, shot_peer(i)[1]), "wait_recv")
+        total[pair_of(shot)] = jnp.sum(arrived[...], axis=0)
+        shots_do(lambda i: sum_copy(i, shot), "start")
 
     send_traces().wait_send()
 
@@ -475,54 +474,35 @@
         each(sends_x, x_copy, t, "wait_send")
         each(sends_y, y_copy, t, "wait_send")
     rows_do("wait_send")
-    edges_do("wait_send")
-
-    def wait_sum(r, carry):
-        @pl.when(r != shot)
+    twin_copy().wait_send()
+    for owner in OWNERS:
+        @pl.when(owner != shot)
         def _():
-            sum_copy(1, r, as_sem).wait_recv()
-        return carry
-
-    lax.fori_loop(2, SHOTS - 2, wait_sum, 0)
-    for e, r in enumerate(EDGE_ROWS):
-        @pl.when(shot != 6 + e)
-        def _():
-            sum_copy(1, r, as_sem).wait_recv()
-
-    last = pltpu.make_async_copy(total, grad_o, out_sem.at[4])
-    last.start()
-    for copy in outs:
-        copy.wait()
+            sum_copy(1, owner).wait_recv()
+    shots_do(lambda i: late_copy(i, shot_peer(i)[1]), "wait_recv")
+    every = late_rows[...].reshape(SHOTS // 2, 2, 8, HALF)
+    total[pl.ds(late, 2)] = jnp.sum(every, axis=0)
+
+    grad_o[...] = total[...]
+
+    shots_do(lambda i: late_copy(i, shot), "wait_send")
 
     @pl.when(owns)
     def _():
-        sums_do(shot, as_sem, "wait_send")
-
-    @pl.when(owns_edge)
-    def _():
-        sums_do(edge_row, bs_sem, "wait_send")
-
-    last.wait()
-
-
-def hand_over(prev_i, cur_i, grad_i, prev_o, cur_o, grad_o, held, held_grad, in_sem, out_sem):
-    steps = []
+        shots_do(lambda i: sum_copy(i, shot), "wait_send")
+
+
+def hand_over(prev_i, cur_i, grad_i, prev_o, cur_o, grad_o, sem):
+    copies = []
     for n in range(2 * PARTS):
         src, dst = ((prev_i, prev_o), (cur_i, cur_o))[n // PARTS]
         part = pl.ds(n % PARTS * (CX // PARTS), CX // PARTS)
-        steps.append((
-            pltpu.make_async_copy(src.at[part], held.at[n], in_sem.at[n]),
-            pltpu.make_async_copy(held.at[n], dst.at[part], out_sem.at[n])))
-    steps.append((
-        pltpu.make_async_copy(grad_i, held_grad, in_sem.at[2 * PARTS]),
-        pltpu.make_async_copy(held_grad, grad_o, out_sem.at[2 * PARTS])))
-    for get, _ in steps:
-        get.start()
-    for get, put in steps:
-        get.wait()
-        put.start()
-    for _, put in steps:
-        put.wait()
+        copies.append(pltpu.make_async_copy(src.at[part], dst.at[part], sem.at[n]))
+    copies.append(pltpu.make_async_copy(grad_i, grad_o, sem.at[2 * PARTS]))
+    for copy in copies:
+        copy.start()
+    for copy in copies:
+        copy.wait()
 
 
 def local_part(adj_prev, adj_cur, fwd_accel, courant2, traces, weights, rblock, column, counts):
@@ -538,8 +518,8 @@
     made = pl.pallas_call(
         kernel,
         out_shape=results,
-        in_specs=[any_] * 8 + [pl.BlockSpec(memory_space=pltpu.HBM)],
-        out_specs=(any_, any_, any_),
+        in_specs=[any_] * 9,
+        out_specs=(vmem, vmem, vmem),
         scratch_shapes=[
             pltpu.VMEM((STEPS + 1, 2, CX + 8, 32, HALF), F32),
             pltpu.VMEM((2, CX, CY, HALF), F32),
@@ -565,19 +545,19 @@
             pltpu.VMEM((128, 1024), BF16),
             pltpu.VMEM((CX * CY, 2 * SLOTS), BF16),
             pltpu.VMEM((SLOTS, 32), F32),
-            pltpu.VMEM((192, HALF), F32),
+            pltpu.VMEM((224, HALF), F32),
             pltpu.VMEM((CX // 2, 8, HALF), F32),
-            pltpu.VMEM((SHOTS, 8, HALF), F32),
+            pltpu.VMEM((SHOTS, 2, 8, HALF), F32),
+            pltpu.VMEM((8, HALF), F32),
             pltpu.VMEM((SHOTS, 8, HALF), F32),
             pltpu.VMEM((CX // 2, 8, HALF), F32),
-            pltpu.VMEM((2, CX, CY, HALF), F32),
             dma((13,)),
             dma((STEPS, 2)), dma((STEPS, 2)), dma((STEPS, 2)), dma((STEPS, 2)),
             dma((1,)), dma((1,)), dma((16,)), dma((16,)),
-            dma((SHOTS,)), dma((SHOTS,)), dma((4,)), dma((SHOTS,)), dma((SHOTS,)), dma((SHOTS,)), dma((SHOTS,)), dma((5,)),
+            dma((SHOTS,)), dma((SHOTS,)), dma((1,)), dma((1,)), dma((SHOTS,)), dma((SHOTS,)), dma((SHOTS,)), dma((SHOTS,)),
         ],
         compiler_params=pltpu.CompilerParams(
-            collective_id=0, has_side_effects=True, vmem_limit_bytes=56 << 20),
+            collective_id=0, has_side_effects=True, vmem_limit_bytes=53760 << 10),
     )(
         adj_prev[0], adj_cur[0], fwd_accel[0], courant2, weights[0, 0].reshape(SLOTS * RB, 256),
         traces, rblock[0], column[0], counts,
@@ -585,14 +565,10 @@
     previous, current, gradient = pl.pallas_call(
         hand_over,
         out_shape=results,
-        in_specs=[any_] * 3,
+        in_specs=[vmem] * 3,
         out_specs=(any_,) * 3,
-        scratch_shapes=[
-            pltpu.VMEM((2 * PARTS, CX // PARTS, CY, 2 * HALF), F32),
-            pltpu.VMEM((CX // 2, CY // 2, HALF), F32),
-            dma((2 * PARTS + 1,)), dma((2 * PARTS + 1,)),
-        ],
-        compiler_params=pltpu.CompilerParams(vmem_limit_bytes=56 << 20),
+        scratch_shapes=[dma((2 * PARTS + 1,))],
+        compiler_params=pltpu.CompilerParams(vmem_limit_bytes=16 << 20),
     )(*made)
     return previous[None], current[None], gradient
 

time: 69.6 us -> 67.6 us (0.971)
  Pallas kernels: 68.1 us -> 65.5 us
    pallas_call x2, Pallas kernels: 68.1 us -> 65.5 us  [the longest x1 64.4 us: local_part(): pl.pallas_call(kernel, out_shape=results, in_specs=[any_] * 9, out_specs=...]
where the time goes in v3:
time: 67.6 us; the launch traced here: 67.5 us
  Pallas kernels  65.5 us (97%)
  between operations  1.31 us (2%)
    pallas_call x1, Pallas kernels, local_part(): pl.pallas_call(kernel, out_shape=results, in_specs=[any_] * 9, out_specs=...  64.4 us

profile of v3, /device:TPU:25, one launch (start us, length us, event | category | flops | bytes accessed | tf_op | source)
XLA Modules:
  0.0 67.5 jit_solution(16053012919539753491)
XLA Ops:
  1.3 0.0 copy-start.2
  1.3 0.0 copy-start
  1.3 0.0 copy-start.1
  1.3 0.6 copy-done.2
  1.9 0.0 copy-done
  2.0 0.0 copy-done.1
  2.0 64.4 %shard_map.112 = (f32[32,16,256]{2,1,0:T(8,128)S(1)}, f32[32,16,256]{2,1,0:T(8,128)S(1)}, f32[16,8,128]{2,1,0:T(8,128)S(1)}) custom-call(f32[32,16,256]{2,1,0:T(8,128)} %bitcast.11, f32[32,16,256]{2,1,0:T(8,128)} %bitcast.12, bf16[4,32,16,256]{3,2,1,0:T(8,128)(2,1)} %bitcast.10, f32[32,16,256]{2,1,0:T(8,128)} %c2_h.1, bf16[1024,256]{1,0:T(8,128)(2,1)} %bitcast.13, ...), custom_call_target="tpu_custom_call" | custom-call | tf_op jit(solution)/shard_map/pallas_call | solution.py:518
  66.4 1.1 %shard_map.113 = (f32[32,16,256]{2,1,0:T(8,128)}, f32[32,16,256]{2,1,0:T(8,128)}, f32[16,8,128]{2,1,0:T(8,128)}) custom-call(f32[32,16,256]{2,1,0:T(8,128)S(1)} %get-tuple-element.9.prev_i, f32[32,16,256]{2,1,0:T(8,128)S(1)} %get-tuple-element.10.cur_i, f32[16,8,128]{2,1,0:T(8,128)S(1)} %get-tuple-element.11.grad_i), custom_call_target="tpu_custom_call" | custom-call | tf_op jit(solution)/shard_map/pallas_call | solution.py:565
Async XLA Ops:
  1.3 0.7 copy-start.2
  1.3 0.7 %copy-start = (bf16[1,4,64]{2,1,0:T(4,128)(2,1)S(1)}, bf16[1,4,64]{2,1,0:T(4,128)(2,1)}, u32[]{:S(2)}) copy-start(bf16[1,4,64]{2,1,0:T(4,128)(2,1)} %tr_h.1) | copy-start | bytes 1540
  1.3 0.7 %copy-start.1 = (s32[1,1,64]{2,1,0:T(1,128)S(1)}, s32[1,1,64]{2,1,0:T(1,128)}, u32[]{:S(2)}) copy-start(s32[1,1,64]{2,1,0:T(1,128)} %param.15) | copy-start | bytes 772

commit v4 on v3

--- a/solution.py
+++ b/solution.py
@@ -173,15 +173,20 @@
             send_sem=xs_sem.at[t, side], recv_sem=xr_sem.at[t, side],
             device_id={"gx": gx + 1 if side == LO else gx - 1}, device_id_type=MESH)
 
-    def y_copy(t, side):
+    PIECES = ((4, CX - 8), (0, 4), (CX - 4, 4))
+
+    def y_copy(t, side, piece):
+        first, planes = PIECES[piece]
+        inner = pl.ds(4 + first, planes)
+        outer = pl.ds(first, planes)
         if side == LO:
-            src = field.at[t, :, pl.ds(4, CX), pl.ds(20, 4), :]
-            dst = halo_y_lo.at[t, :, :, pl.ds(4, 4), :]
+            src = field.at[t, :, inner, pl.ds(20, 4), :]
+            dst = halo_y_lo.at[t, :, outer, pl.ds(4, 4), :]
         else:
-            src = field.at[t, :, pl.ds(4, CX), pl.ds(8, 4), :]
-            dst = halo_y_hi.at[t, :, :, pl.ds(8, 4), :]
-        return pltpu.make_async_remote_copy(
-            src_ref=src, dst_ref=dst, send_sem=ys_sem.at[t, side], recv_sem=yr_sem.at[t, side],
+            src = field.at[t, :, inner, pl.ds(8, 4), :]
+            dst = halo_y_hi.at[t, :, outer, pl.ds(8, 4), :]
+        return pltpu.make_async_remote_copy(
+            src_ref=src, dst_ref=dst, send_sem=ys_sem.at[t, side, piece], recv_sem=yr_sem.at[t, side, piece],
             device_id={"gy": gy + 1 if side == LO else gy - 1}, device_id_type=MESH)
 
     sends_x = {LO: gx < GX - 1, HI: gx > 0}
@@ -194,6 +199,12 @@
             @pl.when(conditions[side])
             def _():
                 getattr(make(t, side), act)()
+
+    def each_y(conditions, pieces, t, act):
+        for piece in pieces:
+            each(conditions, lambda step, side, piece=piece: y_copy(step, side, piece), t, act)
+
+    MIDDLE, OUTER, ALL = (0,), (1, 2), (0, 1, 2)
 
     EDGES = (0, 1, 2, 3, CX - 4, CX - 3, CX - 2, CX - 1)
     for half in range(2):
@@ -318,7 +329,7 @@
 
     send_traces().start()
     each(sends_x, x_copy, 0, "start")
-    each(sends_y, y_copy, 0, "start")
+    each_y(sends_y, ALL, 0, "start")
     get_traces().wait_recv()
 
     def start_trace(i, carry):
@@ -383,11 +394,26 @@
             src_ref=local.at[late + 1 - core], dst_ref=from_twin,
             send_sem=es_sem.at[0], recv_sem=er_sem.at[0], device_id=twin, device_id_type=MESH)
 
+    def late_peer(i):
+        return lax.rem(shot + 2 * i, SHOTS)
+
     def late_copy(i, source_shot):
-        peer, _ = shot_peer(i)
-        return pltpu.make_async_remote_copy(
-            src_ref=late_rows.at[source_shot], dst_ref=late_rows.at[source_shot],
-            send_sem=bs_sem.at[i], recv_sem=br_sem.at[source_shot], device_id=peer, device_id_type=MESH)
+        chip = lax.div(source_shot, 2)
+        return pltpu.make_async_remote_copy(
+            src_ref=late_rows.at[chip], dst_ref=late_rows.at[chip],
+            send_sem=bs_sem.at[i], recv_sem=br_sem.at[chip], device_id={"shot": late_peer(i)}, device_id_type=MESH)
+
+    def swap_copy(which):
+        return pltpu.make_async_remote_copy(
+            src_ref=total.at[late + which], dst_ref=total.at[late + which],
+            send_sem=es_sem.at[1], recv_sem=er_sem.at[1], device_id=twin, device_id_type=MESH)
+
+    def chips_do(make, act):
+        def one(i, carry):
+            getattr(make(i), act)()
+            return carry
+
+        lax.fori_loop(1, SHOTS // 2, one, 0)
 
     def rows_do(act):
         for owner in OWNERS:
@@ -403,22 +429,26 @@
         lax.fori_loop(1, SHOTS, one, 0)
 
     for t in range(STEPS - 1):
-        each(gets_y, y_copy, t, "wait_recv")
+        each_y(gets_y, MIDDLE, t, "wait_recv")
         if t > 0:
             fix_middle(t)
+            each_y(sends_y, MIDDLE, t + 1, "start")
+        each_y(gets_y, OUTER, t, "wait_recv")
         each(gets_x, x_copy, t, "wait_recv")
         fix_edges(t, LO)
         fix_edges(t, HI)
         each(sends_x, x_copy, t + 1, "start")
+        each_y(sends_y, OUTER, t + 1, "start")
         if t == 0:
             fix_middle(t)
-        each(sends_y, y_copy, t + 1, "start")
+            each_y(sends_y, MIDDLE, t + 1, "start")
         make_source(t + 1)
         base_step(t + 1)
 
     t = STEPS - 1
-    each(gets_y, y_copy, t, "wait_recv")
+    each_y(gets_y, MIDDLE, t, "wait_recv")
     fix_middle(t)
+    each_y(gets_y, OUTER, t, "wait_recv")
 
     def edge(side):
         @pl.when(gets_x[side])
@@ -453,8 +483,8 @@
 
     twin_copy().start()
     twin_copy().wait_recv()
-    late_rows[shot] = local[late + core] + from_twin[...]
-    shots_do(lambda i: late_copy(i, shot), "start")
+    late_rows[lax.div(shot, 2)] = local[late + core] + from_twin[...]
+    chips_do(lambda i: late_copy(i, shot), "start")
 
     @pl.when(owns)
     def _():
@@ -472,20 +502,22 @@
     lax.fori_loop(1, 16, end_trace, 0)
     for t in range(STEPS):
         each(sends_x, x_copy, t, "wait_send")
-        each(sends_y, y_copy, t, "wait_send")
+        each_y(sends_y, ALL, t, "wait_send")
     rows_do("wait_send")
     twin_copy().wait_send()
+    chips_do(lambda i: late_copy(i, late_peer(i)), "wait_recv")
+    total[late + core] = jnp.sum(late_rows[...], axis=0)
+    swap_copy(core).start()
     for owner in OWNERS:
         @pl.when(owner != shot)
         def _():
             sum_copy(1, owner).wait_recv()
-    shots_do(lambda i: late_copy(i, shot_peer(i)[1]), "wait_recv")
-    every = late_rows[...].reshape(SHOTS // 2, 2, 8, HALF)
-    total[pl.ds(late, 2)] = jnp.sum(every, axis=0)
+    swap_copy(1 - core).wait_recv()
 
     grad_o[...] = total[...]
 
-    shots_do(lambda i: late_copy(i, shot), "wait_send")
+    chips_do(lambda i: late_copy(i, shot), "wait_send")
+    swap_copy(core).wait_send()
 
     @pl.when(owns)
     def _():
@@ -549,12 +581,12 @@
             pltpu.VMEM((CX // 2, 8, HALF), F32),
             pltpu.VMEM((SHOTS, 2, 8, HALF), F32),
             pltpu.VMEM((8, HALF), F32),
-            pltpu.VMEM((SHOTS, 8, HALF), F32),
+            pltpu.VMEM((SHOTS // 2, 8, HALF), F32),
             pltpu.VMEM((CX // 2, 8, HALF), F32),
             dma((13,)),
-            dma((STEPS, 2)), dma((STEPS, 2)), dma((STEPS, 2)), dma((STEPS, 2)),
+            dma((STEPS, 2)), dma((STEPS, 2)), dma((STEPS, 2, 3)), dma((STEPS, 2, 3)),
             dma((1,)), dma((1,)), dma((16,)), dma((16,)),
-            dma((SHOTS,)), dma((SHOTS,)), dma((1,)), dma((1,)), dma((SHOTS,)), dma((SHOTS,)), dma((SHOTS,)), dma((SHOTS,)),
+            dma((SHOTS,)), dma((SHOTS,)), dma((2,)), dma((2,)), dma((SHOTS,)), dma((SHOTS,)), dma((SHOTS,)), dma((SHOTS,)),
         ],
         compiler_params=pltpu.CompilerParams(
             collective_id=0, has_side_effects=True, vmem_limit_bytes=53760 << 10),

time: 67.6 us -> 66 us (0.976)
  Pallas kernels: 65.5 us -> 63.9 us
    pallas_call x1, Pallas kernels: 64.4 us -> 62.8 us  [local_part(): pl.pallas_call(kernel, out_shape=results, in_specs=[any_] * 9, out_specs=...]
where the time goes in v4:
time: 66 us; the launch traced here: 65.9 us
  Pallas kernels  63.9 us (97%)
  between operations  1.31 us (2%)
  local copies, waits for them, and re-layouts  0.67 us (1%)
    pallas_call x1, Pallas kernels, local_part(): pl.pallas_call(kernel, out_shape=results, in_specs=[any_] * 9, out_specs=...  62.8 us

profile of v4, /device:TPU:25, one launch (start us, length us, event | category | flops | bytes accessed | tf_op | source)
XLA Modules:
  0.0 65.9 jit_solution(16083125428531485509)
XLA Ops:
  1.3 0.0 copy-start.2
  1.3 0.0 copy-start
  1.3 0.0 copy-start.1
  1.3 0.6 copy-done.2
  1.9 0.0 copy-done
  2.0 0.0 copy-done.1
  2.0 62.8 %shard_map.112 = (f32[32,16,256]{2,1,0:T(8,128)S(1)}, f32[32,16,256]{2,1,0:T(8,128)S(1)}, f32[16,8,128]{2,1,0:T(8,128)S(1)}) custom-call(f32[32,16,256]{2,1,0:T(8,128)} %bitcast.11, f32[32,16,256]{2,1,0:T(8,128)} %bitcast.12, bf16[4,32,16,256]{3,2,1,0:T(8,128)(2,1)} %bitcast.10, f32[32,16,256]{2,1,0:T(8,128)} %c2_h.1, bf16[1024,256]{1,0:T(8,128)(2,1)} %bitcast.13, ...), custom_call_target="tpu_custom_call" | custom-call | tf_op jit(solution)/shard_map/pallas_call | solution.py:550
  64.8 1.1 %shard_map.113 = (f32[32,16,256]{2,1,0:T(8,128)}, f32[32,16,256]{2,1,0:T(8,128)}, f32[16,8,128]{2,1,0:T(8,128)}) custom-call(f32[32,16,256]{2,1,0:T(8,128)S(1)} %get-tuple-element.9.prev_i, f32[32,16,256]{2,1,0:T(8,128)S(1)} %get-tuple-element.10.cur_i, f32[16,8,128]{2,1,0:T(8,128)S(1)} %get-tuple-element.11.grad_i), custom_call_target="tpu_custom_call" | custom-call | tf_op jit(solution)/shard_map/pallas_call | solution.py:597
Async XLA Ops:
  1.3 0.7 copy-start.2
  1.3 0.7 %copy-start = (bf16[1,4,64]{2,1,0:T(4,128)(2,1)S(1)}, bf16[1,4,64]{2,1,0:T(4,128)(2,1)}, u32[]{:S(2)}) copy-start(bf16[1,4,64]{2,1,0:T(4,128)(2,1)} %tr_h.1) | copy-start | bytes 1540
  1.3 0.7 %copy-start.1 = (s32[1,1,64]{2,1,0:T(1,128)S(1)}, s32[1,1,64]{2,1,0:T(1,128)}, u32[]{:S(2)}) copy-start(s32[1,1,64]{2,1,0:T(1,128)} %param.15) | copy-start | bytes 772
